TPU v7x, 128 devices: a whole 4x4x4 slice. The times are simulated.
128 devices in a mesh: lon: 16 (over z, y_lo, core), lat: 8 (over x, y_hi).
Axes of the slice: x: 4, y: 4 (y_hi: 2, y_lo: 2; y = y_hi * 2 + y_lo), z: 4, core: 2. Of those that a mesh axis runs over, the one named last changes fastest.
Arguments:
- tokens: bfloat16 [288, 384, 1024], P('lat', 'lon'), may hold values from -6 to 6
- cotangent: bfloat16 [288, 384, 1024], P('lat', 'lon'), may hold values from -6 to 6
- w_qkv: bfloat16 [1024, 3072], replicated, may hold values from -0.1875 to 0.1875
- w_out: bfloat16 [1024, 1024], replicated, may hold values from -0.1875 to 0.1875
- row_valid: int32 [288], replicated, may hold values from 0 to 1, as said below
Outputs:
- d_tokens: bfloat16 [288, 384, 1024], P('lat', 'lon')
- grad_qkv: float32 [1024, 3072], P(('lon', 'lat'))
- grad_out_t: float32 [1024, 1024], P(('lon', 'lat'))
Inputs may be any that keep to these rules, and one draw needn't show every extreme that they name: row_valid is 0 on the first 1 to 3 rows and on the last 1 to 3 rows, and 1 on all other rows.
All inputs are finite; a program needn't handle non-finite values.
Results may differ from a plain program's by a relative error of at most 0.015.
Values may be sent and summed in bfloat16 or wider, within the bound.
A program may use at most 128 MiB of HBM per device.

v0:
```python
import math

import jax
import jax.numpy as jnp
from jax import lax
from jax.sharding import PartitionSpec as P

HEADS = 16
WIN = 6
HEAD_DIM = 64
HALF = 3


COSINE_SHARPNESS = 10.0
EPSILON = 1e-06


def passed_along(value, axis, steps):
    count = lax.axis_size(axis)
    pairs = [(source, (source + steps) % count) for source in range(count)]
    return lax.ppermute(value, axis, pairs)


def window_core(x_win, dy_win, wrap_win, valid_win, w_qkv, w_out):
    win_count, win_area, feature_dim = x_win.shape
    x_float = x_win.reshape(win_count * win_area, feature_dim).astype(jnp.float32)
    inv_rms = lax.rsqrt(jnp.mean(x_float * x_float, axis=-1, keepdims=True) + EPSILON)
    normed = (x_float * inv_rms).astype(jnp.bfloat16)
    qkv_all = jnp.dot(normed, w_qkv, preferred_element_type=jnp.float32).astype(jnp.bfloat16)
    split_heads = qkv_all.reshape(win_count, win_area, 3, HEADS, HEAD_DIM)
    queries = split_heads[:, :, 0].astype(jnp.float32)
    keys_raw = split_heads[:, :, 1].astype(jnp.float32)
    values = split_heads[:, :, 2]
    inv_q = lax.rsqrt(jnp.sum(queries * queries, axis=-1, keepdims=True) + EPSILON)
    inv_k = lax.rsqrt(jnp.sum(keys_raw * keys_raw, axis=-1, keepdims=True) + EPSILON)
    q_unit = queries * inv_q
    k_unit = keys_raw * inv_k
    query_lowprec = q_unit.astype(jnp.bfloat16)
    key_lowprec = k_unit.astype(jnp.bfloat16)
    position = jnp.arange(win_area, dtype=jnp.int32)
    itself = position[:, None] == position[None, :]
    permitted_pairs = (wrap_win[:, :, None] == wrap_win[:, None, :]) & (
        valid_win[:, None, :] | itself[None]
    )
    similarity_scores = COSINE_SHARPNESS * jnp.einsum(
        "sfxe,sqxe->sxfq", query_lowprec, key_lowprec, preferred_element_type=jnp.float32
    )
    unmasked_weights = jnp.where(
        permitted_pairs[:, None], jnp.exp(similarity_scores - COSINE_SHARPNESS), 0.0
    )
    probabilities = unmasked_weights / jnp.sum(unmasked_weights, axis=-1, keepdims=True)
    prob_round = probabilities.astype(jnp.bfloat16)
    attended = jnp.einsum("mxon,mnxq->moxq", prob_round, values, preferred_element_type=jnp.float32)
    attended = attended.astype(jnp.bfloat16).reshape(win_count * win_area, feature_dim)
    dy_flat = dy_win.reshape(win_count * win_area, feature_dim)
    d_att = lax.dot_general(
        dy_flat, w_out, (((1,), (1,)), ((), ())), preferred_element_type=jnp.float32
    )
    d_heads = d_att.astype(jnp.bfloat16).reshape(win_count, win_area, HEADS, HEAD_DIM)
    d_probs = jnp.einsum("sfxe,sqxe->sxfq", d_heads, values, preferred_element_type=jnp.float32)
    d_values = jnp.einsum(
        "vfns,vnfp->vsfp", prob_round, d_heads, preferred_element_type=jnp.float32
    ).astype(jnp.bfloat16)
    d_scores = probabilities * (d_probs - jnp.sum(probabilities * d_probs, axis=-1, keepdims=True))
    grad_scores_lowprec = d_scores.astype(jnp.bfloat16)
    grad_query_direction = COSINE_SHARPNESS * jnp.einsum(
        "mxon,mnxq->moxq", grad_scores_lowprec, key_lowprec, preferred_element_type=jnp.float32
    )
    grad_key_direction = COSINE_SHARPNESS * jnp.einsum(
        "vfns,vnfp->vsfp", grad_scores_lowprec, query_lowprec, preferred_element_type=jnp.float32
    )
    d_queries = (
        inv_q
        * (
            grad_query_direction
            - q_unit * jnp.sum(q_unit * grad_query_direction, axis=-1, keepdims=True)
        )
    ).astype(jnp.bfloat16)
    d_keys = (
        inv_k
        * (
            grad_key_direction
            - k_unit * jnp.sum(k_unit * grad_key_direction, axis=-1, keepdims=True)
        )
    ).astype(jnp.bfloat16)
    d_qkv = jnp.stack([d_queries, d_keys, d_values], axis=2).reshape(
        win_count * win_area, 3 * feature_dim
    )
    d_normed = lax.dot_general(
        d_qkv, w_qkv, (((1,), (1,)), ((), ())), preferred_element_type=jnp.float32
    )
    cubed = inv_rms * inv_rms * inv_rms
    d_input = inv_rms * d_normed - x_float * cubed * jnp.mean(
        d_normed * x_float, axis=-1, keepdims=True
    )
    d_input = d_input.astype(jnp.bfloat16).reshape(win_count, win_area, feature_dim)
    return (d_input, normed, d_qkv, attended, dy_flat)


def to_windows(field_grid):
    groups = field_grid.shape[0] // WIN
    columns = field_grid.shape[1] // WIN
    reshaped = field_grid.reshape((groups, WIN, columns, WIN) + field_grid.shape[2:])
    reordered = jnp.moveaxis(reshaped, 2, 1)
    return reordered.reshape((groups * columns, WIN * WIN) + field_grid.shape[2:])


def on_device(tokens, cotangent, w_qkv, w_out, row_valid):
    lat_dev, lon_dev, feature_dim = tokens.shape
    lat_devices = lax.axis_size("lat")
    lon_devices = lax.axis_size("lon")
    lat_total = lat_dev * lat_devices
    paired = jnp.stack([tokens, cotangent])
    lat_strip = passed_along(paired[:, :HALF], "lat", -1)
    band_block = jnp.concatenate([paired[:, HALF:], lat_strip], axis=1)
    lon_strip = passed_along(band_block[:, :, :HALF], "lon", -1)
    rolled = jnp.concatenate([band_block[:, :, HALF:], lon_strip], axis=2)
    lat_band = lax.axis_index("lat")
    row_index = lat_band * lat_dev + jnp.arange(lat_dev, dtype=jnp.int32)
    anchor = (row_index + HALF) % lat_total
    wrap_rows = anchor < HALF
    shifted_valid = jnp.roll(row_valid, -HALF)
    valid_rows = lax.dynamic_slice_in_dim(shifted_valid, lat_band * lat_dev, lat_dev) == 1
    wrap_grid = jnp.broadcast_to(wrap_rows[:, None], (lat_dev, lon_dev))
    valid_grid = jnp.broadcast_to(valid_rows[:, None], (lat_dev, lon_dev))
    d_win, normed, d_qkv, attended, dy_flat = window_core(
        to_windows(rolled[0]),
        to_windows(rolled[1]),
        to_windows(wrap_grid),
        to_windows(valid_grid),
        w_qkv,
        w_out,
    )
    groups = lat_dev // WIN
    columns = lon_dev // WIN
    d_grid = d_win.reshape(groups, columns, WIN, WIN, feature_dim)
    d_grid = jnp.moveaxis(d_grid, 1, 2).reshape(lat_dev, lon_dev, feature_dim)
    back_rows = passed_along(d_grid[-HALF:], "lat", 1)
    back_block = jnp.concatenate([back_rows, d_grid[:-HALF]], axis=0)
    back_cols = passed_along(back_block[:, -HALF:], "lon", 1)
    d_tokens = jnp.concatenate([back_cols, back_block[:, :-HALF]], axis=1)
    grad_q = lax.dot_general(
        normed, d_qkv, (((0,), (0,)), ((), ())), preferred_element_type=jnp.float32
    )
    grad_o = lax.dot_general(
        dy_flat, attended, (((0,), (0,)), ((), ())), preferred_element_type=jnp.float32
    )
    grad_terms = lax.psum_scatter(
        jnp.concatenate([grad_q, grad_o], axis=1), ("lon", "lat"), scatter_dimension=0, tiled=True
    )
    token_total = lat_dev * lon_dev * lat_devices * lon_devices
    grad_scale = 1.0 / math.sqrt(token_total)
    grad_qkv = grad_terms[:, : 3 * feature_dim] * grad_scale
    grad_out_t = grad_terms[:, 3 * feature_dim :] * grad_scale
    return (d_tokens, grad_qkv, grad_out_t)


def solution(mesh):
    placed = (P("lat", "lon", None), P("lat", "lon", None), P(), P(), P())
    return jax.shard_map(
        on_device,
        mesh=mesh,
        in_specs=placed,
        out_specs=(P("lat", "lon", None), P(("lon", "lat"), None), P(("lon", "lat"), None)),
        check_vma=False,
    )
```

profile of v0, /device:TPU:1, one launch (start us, length us, event | category | flops | bytes accessed | tf_op | source)
XLA Modules:
  0.0 1075.7 jit_solution(11718951915599814820)
XLA Ops:
  7.2 1.2 pad_maximum_fusion.6
  8.4 6.0 collective-permute-start
  14.4 0.7 slice.61
  15.1 0.8 slice.60
  16.5 2.0 fusion.42
  18.5 1.5 collective-permute-done
  20.1 0.2 pad_maximum_fusion.4
  20.3 0.5 copy.48
  20.8 1.6 collective-permute-start.1
  22.4 0.3 or_and_fusion
  22.8 1.0 slice_maximum_fusion
  23.7 5.0 collective-permute-done.1
  28.7 0.2 copy.49
  28.9 3.3 pad_maximum_fusion.3
  32.3 4.8 reshape.133
  37.0 3.0 multiply_reduce_fusion.1
  40.1 0.7 copy-done.2
  40.8 1.8 multiply_convert_fusion.1
  42.6 3.9 reshape_squeeze.4
  46.5 3.4 copy.54
  49.9 3.9 reshape_reshape.7
  53.8 4.7 convolution_convert_fusion.1
  58.6 5.8 reshape.126
  64.5 5.2 copy.51
  69.8 4.9 reshape.130
  74.7 10.4 convolution_convert_fusion
  85.1 13.8 %reshape.125 = bf16[24,36,3,16,64]{4,3,2,1,0:T(8,128)(2,1)} reshape(bf16[864,3072]{1,0:T(8,128)(2,1)} %convolution_convert_fusion) | data formatting | bytes 10616832 | tf_op jit(solution)/shard_map/reshape | solution.py:30
  98.9 6.4 fusion.65
  105.3 4.4 fusion.11
  109.8 9.1 fusion.17
  118.9 8.6 convert_bitcast_fusion.1
  127.5 9.3 convert_bitcast_fusion
  136.7 12.6 %multiply_reduce_fusion = (f32[24,16,36]{2,1,0:T(8,128)S(1)}, f32[24,16,36,36]{2,3,1,0:T(8,128)}) fusion(f32[24,16,36]{2,1,0:T(8,128)S(1)} %get-tuple-element.8, f32[24,16,36,36]{2,3,1,0:T(8,128)} %get-tuple-element.9, pred[24,36,36]{1,2,0:T(8,128)(4,1)S(1)} %or_and_fusion, bf16[24,36,1,16,64]{4,3,2,1,0:T(8,128)(2,1)} %get-tuple-element.3, ...), kind=kOutput, calls=%fused_computation.23 | convolution fusion | flops 66673152 | bytes 7661952 | tf_op jit(solution)/shard_map/sfxe,sqxe->sxfq/dot_general | solution.py:60
  149.4 6.9 multiply_convert_fusion
  156.3 5.6 fusion.39
  161.9 6.7 fusion.35
  168.6 1.7 copy.61
  170.3 3.9 convert_element_type.99
  174.2 4.6 copy.63
  178.8 6.0 reshape.129
  184.9 6.0 fusion.67
  190.9 82.2 %fusion.48 = bf16[24,36,1,16,64]{4,1,3,0,2:T(8,128)(2,1)S(1)} fusion(f32[24,16,64,36]{2,3,1,0:T(8,128)} %fusion.39, f32[24,36,16]{1,2,0:T(8,128)S(1)} %add_rsqrt_fusion, bf16[24,36,1,16,64]{4,3,2,1,0:T(8,128)(2,1)S(1)} %copy-done.6), kind=kOutput, calls=%fused_computation.59 | output fusion | flops 9745983 | bytes 7133184 | tf_op jit(solution)/shard_map/mul | solution.py:83
  273.2 78.7 %fusion.45 = bf16[24,36,1,16,64]{4,1,3,0,2:T(8,128)(2,1)S(1)} fusion(f32[24,16,64,36]{2,3,1,0:T(8,128)S(1)} %bitcast.122, f32[24,36,16]{1,2,0:T(8,128)S(1)} %add_rsqrt_fusion.1, bf16[24,36,1,16,64]{4,3,2,1,0:T(8,128)(2,1)S(1)} %copy-done.4), kind=kOutput, calls=%fused_computation.58 | output fusion | flops 9745983 | bytes 7133184 | tf_op jit(solution)/shard_map/mul | solution.py:76
  351.9 3.2 pad_maximum_fusion.1
  355.1 4.9 copy.59
  360.1 14.2 %reshape.127 = bf16[864,3072]{1,0:T(8,128)(2,1)} reshape(bf16[24,36,3,16,64]{4,3,2,1,0:T(8,128)(2,1)} %copy.59) | data formatting | bytes 10616832 | tf_op jit(solution)/shard_map/reshape | solution.py:86
  374.3 9.1 fusion.66
  383.5 6.0 pad_maximum_fusion
  389.5 10.2 multiply_reduce_fusion.2
  399.8 0.6 subtract_convert_fusion
  400.4 2.2 reshape_reshape.8
  402.6 3.4 copy.60
  406.0 3.9 reshape.128
  409.9 1.1 slice.79
  411.0 3.1 collective-permute-start.2
  414.0 1.5 slice.80
  415.6 6.8 collective-permute-done.2
  422.4 0.2 pad_maximum_fusion.5
  422.6 0.7 collective-permute-start.3
  423.3 7.6 collective-permute-done.3
  430.9 2.0 fusion.55
  433.0 632.5 %reduce-scatter.2.cloned.1.call-done = f32[8,4096]{1,0:T(8,128)} async-done(((f32[1024,4096]{1,0:T(8,128)}), f32[8,4096]{1,0:T(8,128)}) %reduce-scatter.2.cloned.1.call-update) | async-done | bytes 131088 | tf_op jit(solution)/shard_map/reduce_scatter | solution.py:148
  1065.5 1.4 slice_multiply_fusion.1
  1066.9 1.5 slice_multiply_fusion
  (48 shorter events, 1.0 us)
Async XLA Ops:
  7.2 46.7 %copy-start = (bf16[1024,1024]{1,0:T(8,128)(2,1)S(1)}, bf16[1024,1024]{1,0:T(8,128)(2,1)}, u32[]{:S(2)}) copy-start(bf16[1024,1024]{1,0:T(8,128)(2,1)} %param.8) | copy-start | bytes 6291460
  7.2 1058.3 %reduce-scatter.2.cloned.1.call-start = ((), (), s32[]{:S(2)}) async-start(), calls=%async_computation.1 | async-start | bytes 16908288 | tf_op jit(solution)/shard_map/reduce_scatter | solution.py:148
  8.4 11.7 %collective-permute-start = (bf16[2,3,24,1024]{3,2,1,0:T(8,128)(2,1)S(1)}, bf16[2,3,24,1024]{3,2,1,0:T(8,128)(2,1)S(1)}, u32[]{:S(2)}, u32[]{:S(2)}) collective-permute-start(bf16[2,3,24,1024]{3,2,1,0:T(8,128)(2,1)S(1)} %pad_maximum_fusion.6), channel_id=1, source_target_pairs={{0,7},{1,0},{2,1},{3,2},{4,3},{5,4},{6,5},{7,6},{8,15},{9,8},{10,9... | collective-permute-start | bytes 884744 | tf_op jit(solution)/shard_map/ppermute | solution.py:21
  20.8 7.9 collective-permute-start.1
  37.0 3.8 copy-start.2
  105.3 51.0 %copy-start.3 = (bf16[24,36,1,16,64]{4,3,2,1,0:T(8,128)(2,1)}, bf16[24,36,1,16,64]{4,3,2,1,0:T(8,128)(2,1)S(1)}, u32[]{:S(2)}) copy-start(bf16[24,36,1,16,64]{4,3,2,1,0:T(8,128)(2,1)S(1)} %get-tuple-element.5) | copy-start | bytes 5308420
  105.3 56.6 %copy-start.5 = (bf16[24,36,1,16,64]{4,3,2,1,0:T(8,128)(2,1)}, bf16[24,36,1,16,64]{4,3,2,1,0:T(8,128)(2,1)S(1)}, u32[]{:S(2)}) copy-start(bf16[24,36,1,16,64]{4,3,2,1,0:T(8,128)(2,1)S(1)} %get-tuple-element.4) | copy-start | bytes 5308420
  161.9 6.7 copy-start.8
  178.8 6.0 copy-start.11
  184.9 6.0 copy-start.6
  184.9 88.3 %slice-start = ((s8[7864320]{0:T(1024)(128)(4,1)}), s8[4194304]{0:T(1024)(128)(4,1)S(1)}, s32[]{:S(2)}) async-start(s8[7864320]{0:T(1024)(128)(4,1)} %bitcast.121), calls=%async_computation.2 | async-start | bytes 8388608
  190.9 82.3 %copy-start.4 = (bf16[24,36,1,16,64]{4,3,2,1,0:T(8,128)(2,1)S(1)}, bf16[24,36,1,16,64]{4,3,2,1,0:T(8,128)(2,1)}, u32[]{:S(2)}) copy-start(bf16[24,36,1,16,64]{4,3,2,1,0:T(8,128)(2,1)} %copy-done.3) | copy-start | bytes 5308420
  190.9 82.3 %slice-start.1 = ((s8[7864320]{0:T(1024)(128)(4,1)}), s8[3670016]{0:T(1024)(128)(4,1)S(1)}, s32[]{:S(2)}) async-start(s8[7864320]{0:T(1024)(128)(4,1)} %bitcast.121), calls=%async_computation.3 | async-start | bytes 7340032
  273.2 78.7 %copy-start.10 = (bf16[24,36,1,16,64]{4,1,3,0,2:T(8,128)(2,1)S(1)}, bf16[24,36,1,16,64]{4,1,3,0,2:T(8,128)(2,1)}, u32[]{:S(2)}) copy-start(bf16[24,36,1,16,64]{4,1,3,0,2:T(8,128)(2,1)} %convert_bitcast_fusion.1) | copy-start | bytes 5308420
  360.1 14.3 %copy-start.12 = (bf16[864,1024]{1,0:T(8,128)(2,1)S(1)}, bf16[864,1024]{1,0:T(8,128)(2,1)}, u32[]{:S(2)}) copy-start(bf16[864,1024]{1,0:T(8,128)(2,1)} %convert_element_type.99) | copy-start | bytes 5308420
  374.3 9.1 copy-start.9
  389.5 10.3 copy-start.7
  409.9 658.5 %copy-start.1 = (bf16[1024,1024]{1,0:T(8,128)(2,1)S(1)}, bf16[1024,1024]{1,0:T(8,128)(2,1)}, u32[]{:S(2)}) copy-start(bf16[1024,1024]{1,0:T(8,128)(2,1)} %param.8) | copy-start | bytes 6291460
  411.0 11.4 %collective-permute-start.2 = (bf16[3,24,1024]{2,1,0:T(8,128)(2,1)S(1)}, bf16[3,24,1024]{2,1,0:T(8,128)(2,1)S(1)}, u32[]{:S(2)}, u32[]{:S(2)}) collective-permute-start(bf16[3,24,1024]{2,1,0:T(8,128)(2,1)S(1)} %slice.79), channel_id=1, source_target_pairs={{0,1},{1,2},{2,3},{3,4},{4,5},{5,6},{6,7},{7,0},{8,9},{9,10},{10,1... | collective-permute-start | bytes 442376 | tf_op jit(solution)/shard_map/ppermute | solution.py:21
  422.6 8.3 collective-permute-start.3
Sparse Core Ops, SparseCore 0:
  389.6 675.7 reduce-scatter.1
where the time goes:
time: 1100 us; the launch traced here: 1080 us
  waiting for transfers between devices  653 us (59%)
  other arithmetic  200 us (18%)
  local copies, waits for them, and re-layouts  103 us (9%)
  matrix products  92.4 us (8%)
  between operations  14.8 us (1%)
  starting transfers between devices  11.5 us (1%)
    reduce_scatter x1, waiting for transfers between devices, on_device(): lax.psum_scatter(jnp.concatenate([grad_q, grad_o], axis=1), ('lon', 'lat'...  633 us
    mul x1, other arithmetic, window_core(): k_unit * jnp.sum(k_unit * grad_key_direction, axis=-1, keepdims=True)  82.2 us
    mul x1, other arithmetic, window_core(): q_unit * jnp.sum(q_unit * grad_query_direction, axis=-1, keepdims=True)  78.7 us
  transfers between devices with their start and end apart: 5, of which 5 were waited for; matrix products, arithmetic and copies ran while one was open for 3% of the time, Pallas kernels for 0%

commit v1 on v0

v1 whole, which is shorter than its diff:
```python
import functools
import math

import jax
import jax.numpy as jnp
from jax import lax
from jax.experimental import pallas as pl
from jax.experimental.pallas import tpu as pltpu
from jax.sharding import PartitionSpec as P

D = 1024
HEADS = 16
WIN = 6
HEAD_DIM = 64
HALF = 3
ROWS = 36
COLS = 24
LOCAL = ROWS * COLS
STRIPS = ROWS // WIN
STRIP = WIN * COLS
GROUP = 256
CHUNKS = D // GROUP
GROUP_HEADS = GROUP // HEAD_DIM
STACK = GROUP_HEADS * STRIP

SHARP = 10.0
LOG2E = math.log2(math.e)
EPSILON = 1e-06
BLOCKED = -1e30

F32 = jnp.float32
BF16 = jnp.bfloat16
MESH = pl.DeviceIdType.MESH
NN = (((1,), (0,)), ((), ()))
NT = (((1,), (1,)), ((), ()))
TN = (((0,), (0,)), ((), ()))


def dot(a, b, dims=NN):
    return lax.dot_general(a, b, dims, preferred_element_type=F32)


def head_sums(t, ones):
    hi = t.astype(BF16)
    lo = (t - hi.astype(F32)).astype(BF16)
    return dot(hi, ones) + dot(lo, ones)


def by_head(t):
    lane = lax.broadcasted_iota(jnp.int32, t.shape, 1) // HEAD_DIM
    zero = jnp.zeros_like(t)
    return jnp.concatenate([jnp.where(lane == h, t, zero) for h in range(GROUP_HEADS)], axis=0)


def pick_heads(t):
    lane = lax.broadcasted_iota(jnp.int32, (STRIP, GROUP), 1) // HEAD_DIM
    out = t[:STRIP]
    for h in range(1, GROUP_HEADS):
        out = jnp.where(lane == h, t[h * STRIP : (h + 1) * STRIP], out)
    return out


def prologue(x, cot, normed, normed_t, cot_t, inv_rms):
    def norm_strip(s, _):
        rows = pl.ds(pl.multiple_of(s * STRIP, 16), STRIP)
        xf = x[rows, :].astype(F32)
        inv = lax.rsqrt(jnp.mean(xf * xf, axis=-1, keepdims=True) + EPSILON)
        inv_rms[rows, :] = inv
        normed[rows, :] = (xf * inv).astype(BF16)
        return 0

    lax.fori_loop(0, STRIPS, norm_strip, 0)
    for at in range(0, LOCAL, 128):
        width = min(128, LOCAL - at)
        normed_t[:, at : at + width] = normed[at : at + width, :].T
        cot_t[:, at : at + width] = cot[at : at + width, :].T


def project(p, cot, w_qkv, w_out, normed, qb, kb, vb, dab):
    def part(i, _):
        rows = pl.ds(pl.multiple_of(i * 432, 16), 432)
        base = pl.multiple_of(p * GROUP, GROUP)
        n = normed[rows, :]
        qb[rows, :] = dot(n, w_qkv[:, pl.ds(base, GROUP)]).astype(BF16)
        kb[rows, :] = dot(n, w_qkv[:, pl.ds(base + D, GROUP)]).astype(BF16)
        vb[rows, :] = dot(n, w_qkv[:, pl.ds(base + 2 * D, GROUP)]).astype(BF16)
        dab[rows, :] = dot(cot[rows, :], w_out[pl.ds(base, GROUP), :], NT).astype(BF16)
        return 0

    lax.fori_loop(0, 2, part, 0)


def attend(p, bias, qb, kb, vb, dab, ob, d_qkv):
    row_head = lax.broadcasted_iota(jnp.int32, (GROUP, GROUP), 0) // HEAD_DIM
    col_head = lax.broadcasted_iota(jnp.int32, (GROUP, GROUP), 1) // HEAD_DIM
    ones = jnp.where(row_head == col_head, 1.0, 0.0).astype(BF16)

    def strip(s, _):
        rows = pl.ds(pl.multiple_of(s * STRIP, 16), STRIP)
        base = pl.multiple_of(p * GROUP, GROUP)
        q = qb[rows, :].astype(F32)
        k = kb[rows, :].astype(F32)
        inv_q = lax.rsqrt(head_sums(q * q, ones) + EPSILON)
        inv_k = lax.rsqrt(head_sums(k * k, ones) + EPSILON)
        q_unit = q * inv_q
        k_unit = k * inv_k
        q_heads = by_head(q_unit.astype(BF16))
        k_round = k_unit.astype(BF16)
        v = vb[rows, :]
        da_heads = by_head(dab[rows, :])
        scores = dot(q_heads, k_round, NT).reshape(GROUP_HEADS, STRIP, STRIP)
        weights = jnp.exp2(scores * (SHARP * LOG2E) + bias[s][None])
        total = jnp.sum(weights, axis=-1, keepdims=True)
        probs = weights * (1.0 / total)
        prob_round = probs.astype(BF16).reshape(STACK, STRIP)
        d_probs = dot(da_heads, v, NT).reshape(GROUP_HEADS, STRIP, STRIP)
        mixed = jnp.sum(probs * d_probs, axis=-1, keepdims=True)
        ds_round = (probs * (d_probs - mixed)).astype(BF16).reshape(STACK, STRIP)
        ob[rows, :] = pick_heads(dot(prob_round, v)).astype(BF16)
        d_qkv[rows, pl.ds(base + 2 * D, GROUP)] = dot(prob_round, da_heads, TN).astype(BF16)
        dq_unit = SHARP * pick_heads(dot(ds_round, k_round))
        dk_unit = SHARP * dot(ds_round, q_heads, TN)
        d_q = inv_q * (dq_unit - q_unit * head_sums(q_unit * dq_unit, ones))
        d_k = inv_k * (dk_unit - k_unit * head_sums(k_unit * dk_unit, ones))
        d_qkv[rows, pl.ds(base, GROUP)] = d_q.astype(BF16)
        d_qkv[rows, pl.ds(base + D, GROUP)] = d_k.astype(BF16)
        return 0

    lax.fori_loop(0, STRIPS, strip, 0)


def weight_terms(p, normed_t, cot_t, d_qkv, ob, terms):
    def plane(z, _):
        rows = pl.ds(pl.multiple_of(z * 256, 256), 256)
        base = pl.multiple_of(p * GROUP, GROUP)
        n = normed_t[rows, :]
        g_q = dot(n, d_qkv[:, pl.ds(base, GROUP)])
        g_k = dot(n, d_qkv[:, pl.ds(base + D, GROUP)])
        g_v = dot(n, d_qkv[:, pl.ds(base + 2 * D, GROUP)])
        g_o = dot(cot_t[rows, :], ob[...])
        for unit in range(32):
            y_lo, core, x, y_hi = unit // 16, unit // 8 % 2, unit // 2 % 4, unit % 2
            y = y_hi * 2 + y_lo
            part = slice(unit * 8, unit * 8 + 8)
            first = jnp.concatenate([g_q[part], g_k[part]], axis=0)
            second = jnp.concatenate([g_v[part], g_o[part]], axis=0)
            terms[p, core, 0, x, y, z] = first.astype(BF16)
            terms[p, core, 1, z, y, x] = second.astype(BF16)
        return 0

    lax.fori_loop(0, 4, plane, 0)


def token_grad(x, w_qkv, d_qkv, inv_rms, d_normed, d_x):
    def columns(n, _):
        cols = pl.ds(pl.multiple_of(n * 256, 256), 256)
        d_normed[:, cols] = dot(d_qkv[...], w_qkv[cols, :], NT)
        return 0

    lax.fori_loop(0, D // 256, columns, 0)

    def strip(s, _):
        rows = pl.ds(pl.multiple_of(s * STRIP, 16), STRIP)
        xf = x[rows, :].astype(F32)
        dn = d_normed[rows, :]
        inv = inv_rms[rows, :]
        pull = jnp.mean(dn * xf, axis=-1, keepdims=True) * (inv * inv * inv)
        d_x[rows, :] = (inv * dn - xf * pull).astype(BF16)
        return 0

    lax.fori_loop(0, STRIPS, strip, 0)


def window_kernel(x, cot, w_qkv, w_out, bias, d_x, terms, normed, normed_t, cot_t, inv_rms, qb, kb, vb, dab, ob, d_qkv, d_normed):
    prologue(x, cot, normed, normed_t, cot_t, inv_rms)

    def chunk(p, _):
        project(p, cot, w_qkv, w_out, normed, qb, kb, vb, dab)
        attend(p, bias, qb, kb, vb, dab, ob, d_qkv)
        weight_terms(p, normed_t, cot_t, d_qkv, ob, terms)
        return 0

    lax.fori_loop(0, CHUNKS, chunk, 0)
    token_grad(x, w_qkv, d_qkv, inv_rms, d_normed, d_x)


TERMS = (CHUNKS, 2, 2, 4, 4, 4, 16, GROUP)


def window_call(x, cot, w_qkv, w_out, bias):
    vmem = pl.BlockSpec(memory_space=pltpu.VMEM)
    return pl.pallas_call(
        window_kernel,
        out_shape=(jax.ShapeDtypeStruct((LOCAL, D), BF16), jax.ShapeDtypeStruct(TERMS, BF16)),
        in_specs=[vmem] * 5,
        out_specs=(vmem, vmem),
        scratch_shapes=[
            pltpu.VMEM((LOCAL, D), BF16),
            pltpu.VMEM((D, LOCAL), BF16),
            pltpu.VMEM((D, LOCAL), BF16),
            pltpu.VMEM((LOCAL, 1), F32),
            pltpu.VMEM((LOCAL, GROUP), BF16),
            pltpu.VMEM((LOCAL, GROUP), BF16),
            pltpu.VMEM((LOCAL, GROUP), BF16),
            pltpu.VMEM((LOCAL, GROUP), BF16),
            pltpu.VMEM((LOCAL, GROUP), BF16),
            pltpu.VMEM((LOCAL, 3 * D), BF16),
            pltpu.VMEM((LOCAL, D), F32),
        ],
        compiler_params=pltpu.CompilerParams(vmem_limit_bytes=60 * 1024 * 1024),
        name="windows",
    )(x, cot, w_qkv, w_out, bias)


def place():
    lon, lat = lax.axis_index("lon"), lax.axis_index("lat")
    z, y_lo, core = lon // 4, lon // 2 % 2, lon % 2
    x, y_hi = lat // 2, lat % 2
    return x, y_hi * 2 + y_lo, z, core


def device(x, y, z, core):
    return {"lon": z * 4 + y % 2 * 2 + core, "lat": x * 2 + y // 2}


def axis_peer(axis, step):
    x, y, z, core = place()
    if axis == "x":
        at = (x + step) % 4
        return at, device(at, y, z, core)
    if axis == "y":
        at = (y + step) % 4
        return at, device(x, at, z, core)
    at = (z + step) % 4
    return at, device(x, y, at, core)


ORDERS = (("x", "y", "z"), ("z", "y", "x"))


def greet():
    x, y, z, core = place()
    barrier = pltpu.get_barrier_semaphore()
    pl.semaphore_signal(barrier, inc=1, device_id=device(x, y, z, 1 - core), device_id_type=MESH)
    for axis in "xyz":
        for step in (1, 2, 3):
            _, peer = axis_peer(axis, step)
            pl.semaphore_signal(barrier, inc=1, device_id=peer, device_id_type=MESH)
    pl.semaphore_wait(barrier, 10)


def core_copy(p, terms, got_0, send, recv):
    x, y, z, core = place()
    return pltpu.make_async_remote_copy(
        src_ref=terms.at[p, 1 - core],
        dst_ref=got_0.at[p],
        send_sem=send.at[p, 0, 0],
        recv_sem=recv.at[p, 0, 0],
        device_id=device(x, y, z, 1 - core),
        device_id_type=MESH,
    )


def stage_copy(p, stage, half, step, source, target, send, recv):
    at, peer = axis_peer(ORDERS[half][stage], step)
    slot = 3 * half + step - 1
    return pltpu.make_async_remote_copy(
        src_ref=source.at[p, half, at],
        dst_ref=target.at[p, half, step - 1],
        send_sem=send.at[p, 1 + stage, slot],
        recv_sem=recv.at[p, 1 + stage, slot],
        device_id=peer,
        device_id_type=MESH,
    )


STEPS = [(half, step) for half in (0, 1) for step in (1, 2, 3)]


def my_index(stage, half):
    x, y, z, _ = place()
    return {"x": x, "y": y, "z": z}[ORDERS[half][stage]]


def rs_start(p, terms, got_0, send, recv):
    core_copy(p, terms, got_0, send, recv).start()


def rs_first(p, terms, got_0, sum_0, got_1, send, recv):
    core = place()[3]
    core_copy(p, terms, got_0, send, recv).wait_recv()
    for half in (0, 1):
        for a in range(4):
            sum_0[p, half, a] = terms[p, core, half, a] + got_0[p, half, a]
    for half, step in STEPS:
        stage_copy(p, 0, half, step, sum_0, got_1, send, recv).start()


def rs_next(p, stage, source, got, total, after, send, recv):
    for half, step in STEPS:
        stage_copy(p, stage, half, step, source, got, send, recv).wait_recv()
    for half in (0, 1):
        mine = source[p, half, my_index(stage, half)].astype(F32)
        for i in range(3):
            mine = mine + got[p, half, i].astype(F32)
        total[p, half] = mine.astype(total.dtype)
    if after is not None:
        for half, step in STEPS:
            stage_copy(p, stage + 1, half, step, total, after, send, recv).start()


def rs_finish(terms, got_0, sums, gots, send, recv):
    def one(p, _):
        core_copy(p, terms, got_0, send, recv).wait_send()
        for stage in range(3):
            for half, step in STEPS:
                stage_copy(p, stage, half, step, sums[stage], gots[stage], send, recv).wait_send()
        return 0

    lax.fori_loop(0, CHUNKS, one, 0)


def write_grads(sum_3, grad_qkv, grad_out):
    scale = 1.0 / math.sqrt(LOCAL * 128)
    for p in range(CHUNKS):
        at = p * GROUP
        grad_qkv[:, at : at + GROUP] = sum_3[p, 0, :8, :] * scale
        grad_qkv[:, D + at : D + at + GROUP] = sum_3[p, 0, 8:, :] * scale
        grad_qkv[:, 2 * D + at : 2 * D + at + GROUP] = sum_3[p, 1, :8, :] * scale
        grad_out[:, at : at + GROUP] = sum_3[p, 1, 8:, :] * scale


def scatter_kernel(terms, grad_qkv, grad_out, got_0, sum_0, got_1, sum_1, got_2, sum_2, got_3, sum_3, send, recv):
    greet()

    def loop(body):
        lax.fori_loop(0, CHUNKS, lambda p, _: (body(p), 0)[1], 0)

    loop(lambda p: rs_start(p, terms, got_0, send, recv))
    loop(lambda p: rs_first(p, terms, got_0, sum_0, got_1, send, recv))
    loop(lambda p: rs_next(p, 0, sum_0, got_1, sum_1, got_2, send, recv))
    loop(lambda p: rs_next(p, 1, sum_1, got_2, sum_2, got_3, send, recv))
    loop(lambda p: rs_next(p, 2, sum_2, got_3, sum_3, None, send, recv))
    write_grads(sum_3, grad_qkv, grad_out)
    rs_finish(terms, got_0, (sum_0, sum_1, sum_2), (got_1, got_2, got_3), send, recv)


def scatter_scratch():
    unit = (16, GROUP)
    return [
        pltpu.VMEM((CHUNKS, 2, 4, 4, 4) + unit, BF16),
        pltpu.VMEM((CHUNKS, 2, 4, 4, 4) + unit, BF16),
        pltpu.VMEM((CHUNKS, 2, 3, 4, 4) + unit, BF16),
        pltpu.VMEM((CHUNKS, 2, 4, 4) + unit, BF16),
        pltpu.VMEM((CHUNKS, 2, 3, 4) + unit, BF16),
        pltpu.VMEM((CHUNKS, 2, 4) + unit, BF16),
        pltpu.VMEM((CHUNKS, 2, 3) + unit, BF16),
        pltpu.VMEM((CHUNKS, 2) + unit, F32),
        pltpu.SemaphoreType.DMA((CHUNKS, 4, 6)),
        pltpu.SemaphoreType.DMA((CHUNKS, 4, 6)),
    ]


def scatter_call(terms):
    vmem = pl.BlockSpec(memory_space=pltpu.VMEM)
    return pl.pallas_call(
        scatter_kernel,
        out_shape=(jax.ShapeDtypeStruct((8, 3 * D), F32), jax.ShapeDtypeStruct((8, D), F32)),
        in_specs=[vmem],
        out_specs=(vmem, vmem),
        scratch_shapes=scatter_scratch(),
        compiler_params=pltpu.CompilerParams(
            collective_id=0, has_side_effects=True, vmem_limit_bytes=48 * 1024 * 1024
        ),
        name="scatter",
    )(terms)


def passed_along(value, axes, steps):
    sizes = [lax.axis_size(axis) for axis in axes]
    total = math.prod(sizes)
    pairs = []
    for source in range(total):
        if len(axes) == 1:
            pairs.append((source, (source + steps) % total))
        else:
            first, second = source // sizes[1], source % sizes[1]
            pairs.append((source, (first + steps) % sizes[0] * sizes[1] + (second + steps) % sizes[1]))
    return lax.ppermute(value, axes if len(axes) > 1 else axes[0], pairs)


def pair_bias(row_valid):
    lat_total = row_valid.shape[0]
    lat_band = lax.axis_index("lat")
    row = (lat_band * ROWS + jnp.arange(ROWS, dtype=jnp.int32) + HALF) % lat_total
    wrap = row < HALF
    valid = lax.dynamic_slice_in_dim(jnp.roll(row_valid, -HALF), lat_band * ROWS, ROWS) == 1
    wrap = wrap.reshape(STRIPS, WIN)
    valid = valid.reshape(STRIPS, WIN)
    place_in_row = jnp.arange(COLS, dtype=jnp.int32)
    window = (place_in_row - HALF) % COLS // WIN
    token_row = jnp.repeat(jnp.arange(WIN), COLS)
    token_window = jnp.tile(window, WIN)
    token_wrap = wrap[:, token_row]
    token_valid = valid[:, token_row]
    itself = jnp.eye(STRIP, dtype=bool)
    allowed = (
        (token_window[:, None] == token_window[None, :])[None]
        & (token_wrap[:, :, None] == token_wrap[:, None, :])
        & (token_valid[:, None, :] | itself[None])
    )
    return jnp.where(allowed, -SHARP * LOG2E, BLOCKED).astype(F32)


def on_device(tokens, cotangent, w_qkv, w_out, row_valid):
    paired = jnp.stack([tokens, cotangent])
    below = passed_along(paired[:, :HALF], ("lat",), -1)
    beside = passed_along(paired[:, HALF:, :HALF], ("lon",), -1)
    corner = passed_along(paired[:, :HALF, :HALF], ("lon", "lat"), -1)
    side = jnp.concatenate([beside, corner], axis=1)
    body = jnp.concatenate([paired[:, HALF:, HALF:], below[:, :, HALF:]], axis=1)
    rolled = jnp.concatenate([side, body], axis=2).reshape(2, LOCAL, D)
    d_x, terms = window_call(rolled[0], rolled[1], w_qkv, w_out, pair_bias(row_valid))
    grad_qkv, grad_out = scatter_call(terms)
    d_grid = d_x.reshape(ROWS, COLS, D)
    side = d_grid[:, :HALF]
    from_left = passed_along(side[:-HALF], ("lon",), 1)
    from_above = passed_along(d_grid[-HALF:], ("lat",), 1)
    from_corner = passed_along(side[-HALF:], ("lon", "lat"), 1)
    side = jnp.concatenate([from_corner, from_left], axis=0)
    body = jnp.concatenate([from_above[:, HALF:], d_grid[:-HALF, HALF:]], axis=0)
    d_tokens = jnp.concatenate([side, body], axis=1)
    return (d_tokens, grad_qkv, grad_out)


def solution(mesh):
    placed = (P("lat", "lon", None), P("lat", "lon", None), P(), P(), P())
    return jax.shard_map(
        on_device,
        mesh=mesh,
        in_specs=placed,
        out_specs=(P("lat", "lon", None), P(("lon", "lat"), None), P(("lon", "lat"), None)),
        check_vma=False,
    )
```

time: 1100 us -> 160 us (0.15); the launches traced: 1080 us -> 159 us
  waiting for transfers between devices: 653 us -> 0.02 us
  other arithmetic: 200 us -> 10.9 us
  Pallas kernels: 0 us -> 116 us
  matrix products: 92.4 us -> 0 us
  local copies, waits for them, and re-layouts: 103 us -> 17.8 us
  between operations: 14.8 us -> 0.81 us
    reduce_scatter x1 -> x0, waiting for transfers between devices: 633 us -> none  [on_device(): lax.psum_scatter(jnp.concatenate([grad_q, grad_o], axis=1), ('lon', 'lat'...]
    mul x5 -> x0, other arithmetic: 164 us -> none  [the longest x1 82.2 us: window_core(): k_unit * jnp.sum(k_unit * grad_key_direction, axis=-1, keepdims=True)]
    pallas_call x0 -> x2, Pallas kernels: none -> 116 us  [the longest x1 69.5 us: window_call(): pl.pallas_call(window_kernel, out_shape=(jax.ShapeDtypeStruct((LOCAL, D),...]
    dot_general x11 -> x0, matrix products: 92.4 us -> none  [the longest x1 12.6 us: window_core(): jnp.einsum('sfxe,sqxe->sxfq', d_heads, values, preferred_element_type=jnp...]
    reshape x5 -> x3, local copies, waits for them, and re-layouts: 43.8 us -> 0.85 us  [the longest x1 0.65 us: pair_bias(): token_row = jnp.repeat(jnp.arange(WIN), COLS)]
    convert_element_type x6 -> x0, local copies, waits for them, and re-layouts: 25.1 us -> none  [the longest x3 14.9 us: window_core(): x_win.reshape(win_count * win_area, feature_dim).astype(jnp.float32)]
    ppermute x4 -> x6, waiting for transfers between devices: 20.9 us -> 0.02 us  [passed_along(): return lax.ppermute(value, axes if len(axes) > 1 else axes[0], pairs)]
    another operation x4 -> x1, local copies, waits for them, and re-layouts: 14.9 us -> 0.66 us  [pair_bias(): token_window = jnp.tile(window, WIN)]
  transfers between devices with their start and end apart: 5 -> 6, of which waited for: 5 -> 0; matrix products, arithmetic and copies ran while one was open for 3% -> 11% of each run, Pallas kernels for 0% -> 30%
where the time goes in v1:
time: 160 us; the launch traced here: 159 us
  Pallas kernels  116 us (72%)
  local copies, waits for them, and re-layouts  17.8 us (11%)
  starting transfers between devices  13.3 us (8%)
  other arithmetic  10.9 us (7%)
    pallas_call x1, Pallas kernels, window_call(): pl.pallas_call(window_kernel, out_shape=(jax.ShapeDtypeStruct((LOCAL, D),...  69.5 us
    pallas_call x1, Pallas kernels, scatter_call(): pl.pallas_call(scatter_kernel, out_shape=(jax.ShapeDtypeStruct((8, 3 * D)...  47 us
    ppermute x6, starting transfers between devices, passed_along(): return lax.ppermute(value, axes if len(axes) > 1 else axes[0], pairs)  13.3 us
  transfers between devices with their start and end apart: 6, of which 0 were waited for; matrix products, arithmetic and copies ran while one was open for 11% of the time, Pallas kernels for 30%

profile of v1, /device:TPU:1, one launch (start us, length us, event | category | flops | bytes accessed | tf_op | source)
XLA Modules:
  0.0 159.2 jit_solution(4053333423084687773)
XLA Ops:
  0.6 0.0 copy-start
  0.6 0.0 copy-start.1
  0.7 1.6 %pad_maximum_fusion.2 = bf16[2,3,3,1024]{3,2,1,0:T(4,128)(2,1)} fusion(bf16[1,36,24,1024]{3,2,1,0:T(8,128)(2,1)} %bitcast.9, bf16[1,36,24,1024]{3,2,1,0:T(8,128)(2,1)} %bitcast.13), kind=kLoop, calls=%fused_computation.12 | loop fusion | flops 73728 | bytes 3575808 | tf_op jit(solution)/shard_map/slice | solution.py:419
  2.3 6.5 %collective-permute-start.1 = (bf16[2,3,3,1024]{3,2,1,0:T(4,128)(2,1)}, bf16[2,3,3,1024]{3,2,1,0:T(4,128)(2,1)}, u32[]{:S(2)}, u32[]{:S(2)}) collective-permute-start(bf16[2,3,3,1024]{3,2,1,0:T(4,128)(2,1)} %pad_maximum_fusion.2), channel_id=1, source_target_pairs={{0,127},{1,120},{2,121},{3,122},{4,123},{5,124},{6,125},{7,126},{8... | collective-permute-start | bytes 110600 | tf_op jit(solution)/shard_map/ppermute | solution.py:389
  8.8 0.0 copy-done
  8.8 0.0 copy-done.1
  8.8 0.7 pad_maximum_fusion.1
  9.5 0.0 copy-start.2
  9.5 0.0 slice-start
  9.5 0.1 collective-permute-start.2
  9.6 0.2 pad_maximum_fusion
  9.8 1.1 copy.16
  10.9 3.7 %collective-permute-start = (bf16[2,33,3,1024]{3,0,2,1:T(2,128)(2,1)}, bf16[2,33,3,1024]{3,0,2,1:T(2,128)(2,1)}, u32[]{:S(2)}, u32[]{:S(2)}) collective-permute-start(bf16[2,33,3,1024]{3,0,2,1:T(2,128)(2,1)} %copy.16), channel_id=1, source_target_pairs={{0,120},{8,0},{16,8},{24,16},{32,24},{40,32},{48,40},{56,48},{64,5... | collective-permute-start | bytes 1216520 | tf_op jit(solution)/shard_map/ppermute | solution.py:389
  14.6 0.5 and_select_fusion.1
  15.1 0.0 copy-done.2
  15.1 0.1 slice.59
  15.2 0.0 slice-done
  15.2 0.1 pad_add_fusion
  15.3 0.1 dynamic-slice_compare_fusion
  15.3 0.1 reshape.115
  15.4 0.1 copy.20
  15.5 0.7 tile.2
  16.2 0.1 eq.49
  16.3 0.6 reshape.114
  16.9 0.7 compare_select_fusion
  17.6 1.3 gather_fusion.1
  18.9 0.8 copy.21
  19.7 1.3 gather_fusion
  21.1 0.8 copy.18
  21.9 0.1 iota_compare_fusion
  22.0 1.2 and_select_fusion.bias
  23.2 1.0 fusion
  24.2 0.0 collective-permute-done.2
  24.3 1.0 slice.73
  25.3 0.0 collective-permute-done
  25.3 1.2 copy.17
  26.5 0.0 collective-permute-done.1
  26.5 2.5 %maximum_maximum_fusion = bf16[2,36,24,1024]{3,2,1,0:T(8,128)(2,1)S(1)} fusion(bf16[2,3,21,1024]{3,2,1,0:T(8,128)(2,1)S(1)} %slice.73, bf16[2,33,21,1024]{3,2,1,0:T(8,128)(2,1)S(1)} %fusion, bf16[2,3,3,1024]{3,2,1,0:T(4,128)(2,1)} %collective-permute-done.1, bf16[2,33,3,1024]{3,2,1,0:T(4,128)(2,1)S(1)} %copy.17), kind=kLoop, calls=%fused_computation.4 | loop fusion | flops 14155776 | bytes 7077888 | tf_op jit(solution)/shard_map/concatenate | solution.py:422
  29.1 2.2 %fusion.5 = (bf16[1,36,24,1024]{3,2,1,0:T(8,128)(2,1)}, bf16[1,36,24,1024]{3,2,1,0:T(8,128)(2,1)}) fusion(bf16[2,36,24,1024]{3,2,1,0:T(8,128)(2,1)S(1)} %maximum_maximum_fusion), kind=kLoop, calls=%fused_computation.25 | loop fusion | bytes 7077888 | tf_op jit(solution)/shard_map/slice | solution.py:423
  31.3 69.5 %windows.1 = (bf16[864,1024]{1,0:T(8,128)(2,1)}, bf16[4,2,2,4,4,4,16,256]{7,6,5,4,3,2,1,0:T(8,128)(2,1)}) custom-call(bf16[864,1024]{1,0:T(8,128)(2,1)} %bitcast.18, bf16[864,1024]{1,0:T(8,128)(2,1)} %bitcast.17, bf16[1024,3072]{1,0:T(8,128)(2,1)} %w_qkv.1, bf16[1024,1024]{1,0:T(8,128)(2,1)} %w_out.1, f32[6,144,144]{2,1,0:T(8,128)} %and_select_fusion.bias), custom_call_target="tpu_custom_call" | custom-call | tf_op jit(solution)/shard_map/windows/pallas_call | solution.py:192
  100.8 1.1 slice.77
  101.9 0.1 collective-permute-start.4
  102.0 0.9 slice.63
  102.9 2.7 %collective-permute-start.5 = (bf16[3,24,1024]{2,1,0:T(8,128)(2,1)S(1)}, bf16[3,24,1024]{2,1,0:T(8,128)(2,1)S(1)}, u32[]{:S(2)}, u32[]{:S(2)}) collective-permute-start(bf16[3,24,1024]{2,1,0:T(8,128)(2,1)S(1)} %bitcast.22), channel_id=1, source_target_pairs={{0,1},{1,2},{2,3},{3,4},{4,5},{5,6},{6,7},{7,0},{8,9},{9,10},{10,1... | collective-permute-start | bytes 442376 | tf_op jit(solution)/shard_map/ppermute | solution.py:389
  105.6 0.8 slice.76
  106.4 0.3 collective-permute-start.3
  106.7 2.2 %slice.79 = bf16[33,21,1024]{2,1,0:T(8,128)(2,1)S(1)} slice(bf16[36,24,1024]{2,1,0:T(8,128)(2,1)} %bitcast.21), slice={[0:33], [3:24], [0:1024]} | slice | bytes 2838528 | tf_op jit(solution)/shard_map/slice | solution.py:431
  108.8 47.0 %scatter.1 = (f32[8,3072]{1,0:T(8,128)S(1)}, f32[8,1024]{1,0:T(8,128)S(1)}) custom-call(bf16[4,2,2,4,4,4,16,256]{7,6,5,4,3,2,1,0:T(8,128)(2,1)} %get-tuple-element.8.terms), custom_call_target="tpu_custom_call" | custom-call | tf_op jit(solution)/shard_map/scatter/pallas_call | solution.py:366
  155.8 0.0 collective-permute-done.5
  155.9 0.0 collective-permute-done.3
  155.9 0.0 collective-permute-done.4
  155.9 2.1 %maximum_maximum_fusion.1 = bf16[36,24,1024]{2,1,0:T(8,128)(2,1)} fusion(bf16[33,21,1024]{2,1,0:T(8,128)(2,1)S(1)} %slice.79, bf16[3,21,1024]{2,1,0:T(8,128)(2,1)S(1)} %slice.78, bf16[33,3,1024]{2,1,0:T(4,128)(2,1)S(1)} %collective-permute-done.4, bf16[3,3,1024]{2,1,0:T(4,128)(2,1)S(1)} %collective-permute-done.3), kind=kLoop, calls=%fused_computation.6 | loop fusion | flops 7077888 | bytes 3538944 | tf_op jit(solution)/shard_map/concatenate | solution.py:432
  158.0 0.6 copy.24
  158.6 0.6 copy.25
  (4 shorter events, 0.1 us)
Async XLA Ops:
  0.6 8.1 %copy-start = (bf16[36,24,1024]{2,1,0:T(8,128)(2,1)S(1)}, bf16[36,24,1024]{2,1,0:T(8,128)(2,1)}, u32[]{:S(2)}) copy-start(bf16[36,24,1024]{2,1,0:T(8,128)(2,1)} %param.6) | copy-start | bytes 5308420
  0.6 8.1 %copy-start.1 = (bf16[36,24,1024]{2,1,0:T(8,128)(2,1)S(1)}, bf16[36,24,1024]{2,1,0:T(8,128)(2,1)}, u32[]{:S(2)}) copy-start(bf16[36,24,1024]{2,1,0:T(8,128)(2,1)} %param.5) | copy-start | bytes 5308420
  2.3 24.3 %collective-permute-start.1 = (bf16[2,3,3,1024]{3,2,1,0:T(4,128)(2,1)}, bf16[2,3,3,1024]{3,2,1,0:T(4,128)(2,1)}, u32[]{:S(2)}, u32[]{:S(2)}) collective-permute-start(bf16[2,3,3,1024]{3,2,1,0:T(4,128)(2,1)} %pad_maximum_fusion.2), channel_id=1, source_target_pairs={{0,127},{1,120},{2,121},{3,122},{4,123},{5,124},{6,125},{7,126},{8... | collective-permute-start | bytes 110600 | tf_op jit(solution)/shard_map/ppermute | solution.py:389
  9.5 5.6 %copy-start.2 = (s32[288]{0:T(512)S(1)}, s32[288]{0:T(512)}, u32[]{:S(2)}) copy-start(s32[288]{0:T(512)} %param.9) | copy-start | bytes 3460
  9.5 5.7 %slice-start = ((s32[288]{0:T(512)}), s32[3]{0:T(128)S(1)}, s32[]{:S(2)}) async-start(s32[288]{0:T(512)} %param.9), calls=%async_computation | async-start | bytes 1024 | tf_op jit(solution)/shard_map/jit(_roll_static)/slice | solution.py:397
  9.5 14.7 %collective-permute-start.2 = (bf16[2,3,24,1024]{3,2,1,0:T(8,128)(2,1)}, bf16[2,3,24,1024]{3,2,1,0:T(8,128)(2,1)}, u32[]{:S(2)}, u32[]{:S(2)}) collective-permute-start(bf16[2,3,24,1024]{3,2,1,0:T(8,128)(2,1)} %pad_maximum_fusion.1), channel_id=1, source_target_pairs={{0,7},{1,0},{2,1},{3,2},{4,3},{5,4},{6,5},{7,6},{8,15},{9,8},{10,9... | collective-permute-start | bytes 884744 | tf_op jit(solution)/shard_map/ppermute | solution.py:389
  10.9 14.4 %collective-permute-start = (bf16[2,33,3,1024]{3,0,2,1:T(2,128)(2,1)}, bf16[2,33,3,1024]{3,0,2,1:T(2,128)(2,1)}, u32[]{:S(2)}, u32[]{:S(2)}) collective-permute-start(bf16[2,33,3,1024]{3,0,2,1:T(2,128)(2,1)} %copy.16), channel_id=1, source_target_pairs={{0,120},{8,0},{16,8},{24,16},{32,24},{40,32},{48,40},{56,48},{64,5... | collective-permute-start | bytes 1216520 | tf_op jit(solution)/shard_map/ppermute | solution.py:389
  101.9 54.0 %collective-permute-start.4 = (bf16[33,3,1024]{2,1,0:T(4,128)(2,1)S(1)}, bf16[33,3,1024]{2,1,0:T(4,128)(2,1)S(1)}, u32[]{:S(2)}, u32[]{:S(2)}) collective-permute-start(bf16[33,3,1024]{2,1,0:T(4,128)(2,1)S(1)} %slice.77), channel_id=1, source_target_pairs={{0,8},{8,16},{16,24},{24,32},{32,40},{40,48},{48,56},{56,64},{64,7... | collective-permute-start | bytes 608264 | tf_op jit(solution)/shard_map/ppermute | solution.py:389
  102.9 52.9 %collective-permute-start.5 = (bf16[3,24,1024]{2,1,0:T(8,128)(2,1)S(1)}, bf16[3,24,1024]{2,1,0:T(8,128)(2,1)S(1)}, u32[]{:S(2)}, u32[]{:S(2)}) collective-permute-start(bf16[3,24,1024]{2,1,0:T(8,128)(2,1)S(1)} %bitcast.22), channel_id=1, source_target_pairs={{0,1},{1,2},{2,3},{3,4},{4,5},{5,6},{6,7},{7,0},{8,9},{9,10},{10,1... | collective-permute-start | bytes 442376 | tf_op jit(solution)/shard_map/ppermute | solution.py:389
  106.4 49.5 %collective-permute-start.3 = (bf16[3,3,1024]{2,1,0:T(4,128)(2,1)S(1)}, bf16[3,3,1024]{2,1,0:T(4,128)(2,1)S(1)}, u32[]{:S(2)}, u32[]{:S(2)}) collective-permute-start(bf16[3,3,1024]{2,1,0:T(4,128)(2,1)S(1)} %slice.76), channel_id=1, source_target_pairs={{0,9},{1,10},{2,11},{3,12},{4,13},{5,14},{6,15},{7,8},{8,17},{9,18... | collective-permute-start | bytes 55304 | tf_op jit(solution)/shard_map/ppermute | solution.py:389

commit v2 on v1

--- a/solution.py
+++ b/solution.py
@@ -151,14 +151,12 @@
     lax.fori_loop(0, 4, plane, 0)
 
 
-def token_grad(x, w_qkv, d_qkv, inv_rms, d_normed, d_x):
-    def columns(n, _):
-        cols = pl.ds(pl.multiple_of(n * 256, 256), 256)
-        d_normed[:, cols] = dot(d_qkv[...], w_qkv[cols, :], NT)
-        return 0
-
-    lax.fori_loop(0, D // 256, columns, 0)
-
+def normed_grad(n, w_qkv, d_qkv, d_normed):
+    cols = pl.ds(pl.multiple_of(n * 256, 256), 256)
+    d_normed[:, cols] = dot(d_qkv[...], w_qkv[cols, :], NT)
+
+
+def token_grad(x, inv_rms, d_normed, d_x):
     def strip(s, _):
         rows = pl.ds(pl.multiple_of(s * STRIP, 16), STRIP)
         xf = x[rows, :].astype(F32)
@@ -171,30 +169,77 @@
     lax.fori_loop(0, STRIPS, strip, 0)
 
 
-def window_kernel(x, cot, w_qkv, w_out, bias, d_x, terms, normed, normed_t, cot_t, inv_rms, qb, kb, vb, dab, ob, d_qkv, d_normed):
+def pair_bias(invalid, bias):
+    query = lax.broadcasted_iota(jnp.int32, (STRIP, STRIP), 0)
+    key = lax.broadcasted_iota(jnp.int32, (STRIP, STRIP), 1)
+    window = lambda t: (t % COLS + COLS - HALF) % COLS // WIN
+    half = lambda t: t // (HALF * COLS)
+    same_window = window(query) == window(key)
+    same_half = half(query) == half(key)
+    seam = lax.axis_index("lat") == lax.axis_size("lat") - 1
+    open_bias = jnp.where(same_window, -SHARP * LOG2E, BLOCKED)
+    seam_bias = jnp.where(same_window & same_half, -SHARP * LOG2E, BLOCKED)
+    others = jnp.where(query == key, 0.0, BLOCKED)
+    for s in range(STRIPS):
+        base = open_bias if s < STRIPS - 1 else jnp.where(seam, seam_bias, open_bias)
+        bias[s] = base + others * invalid[s : s + 1, :]
+
+
+def window_kernel(
+    x, cot, w_qkv, w_out, invalid, d_x, grad_qkv, grad_out,
+    bias, normed, normed_t, cot_t, inv_rms, qb, kb, vb, dab, ob, d_qkv, d_normed, terms,
+    got_0, sum_0, got_1, sum_1, got_2, sum_2, got_3, sum_3, send, recv,
+):
+    greet()
+    pair_bias(invalid, bias)
     prologue(x, cot, normed, normed_t, cot_t, inv_rms)
+    first = lambda p: rs_first(p, terms, got_0, sum_0, got_1, send, recv)
+    second = lambda p: rs_next(p, 0, sum_0, got_1, sum_1, got_2, send, recv)
+    third = lambda p: rs_next(p, 1, sum_1, got_2, sum_2, got_3, send, recv)
+    last = lambda p: rs_next(p, 2, sum_2, got_3, sum_3, None, send, recv)
 
     def chunk(p, _):
         project(p, cot, w_qkv, w_out, normed, qb, kb, vb, dab)
+        pl.when(p > 0)(lambda: first(p - 1))
         attend(p, bias, qb, kb, vb, dab, ob, d_qkv)
+        pl.when(p > 0)(lambda: second(p - 1))
         weight_terms(p, normed_t, cot_t, d_qkv, ob, terms)
+        rs_start(p, terms, got_0, send, recv)
+        pl.when(p > 0)(lambda: third(p - 1))
         return 0
 
     lax.fori_loop(0, CHUNKS, chunk, 0)
-    token_grad(x, w_qkv, d_qkv, inv_rms, d_normed, d_x)
+
+    def tail(n, _):
+        normed_grad(n, w_qkv, d_qkv, d_normed)
+        pl.when(n == 0)(lambda: first(CHUNKS - 1))
+        pl.when(n == 3)(lambda: second(CHUNKS - 1))
+        return 0
+
+    lax.fori_loop(0, D // 256, tail, 0)
+    token_grad(x, inv_rms, d_normed, d_x)
+    third(CHUNKS - 1)
+    lax.fori_loop(0, CHUNKS, lambda p, _: (last(p), 0)[1], 0)
+    write_grads(sum_3, grad_qkv, grad_out)
+    rs_finish(terms, got_0, (sum_0, sum_1, sum_2), (got_1, got_2, got_3), send, recv)
 
 
 TERMS = (CHUNKS, 2, 2, 4, 4, 4, 16, GROUP)
 
 
-def window_call(x, cot, w_qkv, w_out, bias):
+def window_call(x, cot, w_qkv, w_out, invalid):
     vmem = pl.BlockSpec(memory_space=pltpu.VMEM)
     return pl.pallas_call(
         window_kernel,
-        out_shape=(jax.ShapeDtypeStruct((LOCAL, D), BF16), jax.ShapeDtypeStruct(TERMS, BF16)),
+        out_shape=(
+            jax.ShapeDtypeStruct((LOCAL, D), BF16),
+            jax.ShapeDtypeStruct((8, 3 * D), F32),
+            jax.ShapeDtypeStruct((8, D), F32),
+        ),
         in_specs=[vmem] * 5,
-        out_specs=(vmem, vmem),
+        out_specs=(vmem, vmem, vmem),
         scratch_shapes=[
+            pltpu.VMEM((STRIPS, STRIP, STRIP), F32),
             pltpu.VMEM((LOCAL, D), BF16),
             pltpu.VMEM((D, LOCAL), BF16),
             pltpu.VMEM((D, LOCAL), BF16),
@@ -206,10 +251,14 @@
             pltpu.VMEM((LOCAL, GROUP), BF16),
             pltpu.VMEM((LOCAL, 3 * D), BF16),
             pltpu.VMEM((LOCAL, D), F32),
-        ],
-        compiler_params=pltpu.CompilerParams(vmem_limit_bytes=60 * 1024 * 1024),
+            pltpu.VMEM(TERMS, BF16),
+        ]
+        + scatter_scratch(),
+        compiler_params=pltpu.CompilerParams(
+            collective_id=0, has_side_effects=True, vmem_limit_bytes=60 * 1024 * 1024
+        ),
         name="windows",
-    )(x, cot, w_qkv, w_out, bias)
+    )(x, cot, w_qkv, w_out, invalid)
 
 
 def place():
@@ -328,21 +377,6 @@
         grad_qkv[:, D + at : D + at + GROUP] = sum_3[p, 0, 8:, :] * scale
         grad_qkv[:, 2 * D + at : 2 * D + at + GROUP] = sum_3[p, 1, :8, :] * scale
         grad_out[:, at : at + GROUP] = sum_3[p, 1, 8:, :] * scale
-
-
-def scatter_kernel(terms, grad_qkv, grad_out, got_0, sum_0, got_1, sum_1, got_2, sum_2, got_3, sum_3, send, recv):
-    greet()
-
-    def loop(body):
-        lax.fori_loop(0, CHUNKS, lambda p, _: (body(p), 0)[1], 0)
-
-    loop(lambda p: rs_start(p, terms, got_0, send, recv))
-    loop(lambda p: rs_first(p, terms, got_0, sum_0, got_1, send, recv))
-    loop(lambda p: rs_next(p, 0, sum_0, got_1, sum_1, got_2, send, recv))
-    loop(lambda p: rs_next(p, 1, sum_1, got_2, sum_2, got_3, send, recv))
-    loop(lambda p: rs_next(p, 2, sum_2, got_3, sum_3, None, send, recv))
-    write_grads(sum_3, grad_qkv, grad_out)
-    rs_finish(terms, got_0, (sum_0, sum_1, sum_2), (got_1, got_2, got_3), send, recv)
 
 
 def scatter_scratch():
@@ -361,21 +395,6 @@
     ]
 
 
-def scatter_call(terms):
-    vmem = pl.BlockSpec(memory_space=pltpu.VMEM)
-    return pl.pallas_call(
-        scatter_kernel,
-        out_shape=(jax.ShapeDtypeStruct((8, 3 * D), F32), jax.ShapeDtypeStruct((8, D), F32)),
-        in_specs=[vmem],
-        out_specs=(vmem, vmem),
-        scratch_shapes=scatter_scratch(),
-        compiler_params=pltpu.CompilerParams(
-            collective_id=0, has_side_effects=True, vmem_limit_bytes=48 * 1024 * 1024
-        ),
-        name="scatter",
-    )(terms)
-
-
 def passed_along(value, axes, steps):
     sizes = [lax.axis_size(axis) for axis in axes]
     total = math.prod(sizes)
@@ -389,27 +408,9 @@
     return lax.ppermute(value, axes if len(axes) > 1 else axes[0], pairs)
 
 
-def pair_bias(row_valid):
-    lat_total = row_valid.shape[0]
-    lat_band = lax.axis_index("lat")
-    row = (lat_band * ROWS + jnp.arange(ROWS, dtype=jnp.int32) + HALF) % lat_total
-    wrap = row < HALF
-    valid = lax.dynamic_slice_in_dim(jnp.roll(row_valid, -HALF), lat_band * ROWS, ROWS) == 1
-    wrap = wrap.reshape(STRIPS, WIN)
-    valid = valid.reshape(STRIPS, WIN)
-    place_in_row = jnp.arange(COLS, dtype=jnp.int32)
-    window = (place_in_row - HALF) % COLS // WIN
-    token_row = jnp.repeat(jnp.arange(WIN), COLS)
-    token_window = jnp.tile(window, WIN)
-    token_wrap = wrap[:, token_row]
-    token_valid = valid[:, token_row]
-    itself = jnp.eye(STRIP, dtype=bool)
-    allowed = (
-        (token_window[:, None] == token_window[None, :])[None]
-        & (token_wrap[:, :, None] == token_wrap[:, None, :])
-        & (token_valid[:, None, :] | itself[None])
-    )
-    return jnp.where(allowed, -SHARP * LOG2E, BLOCKED).astype(F32)
+def invalid_keys(row_valid):
+    rows = lax.dynamic_slice_in_dim(jnp.roll(row_valid, -HALF), lax.axis_index("lat") * ROWS, ROWS)
+    return jnp.repeat(1.0 - rows.astype(F32), COLS).reshape(STRIPS, STRIP)
 
 
 def on_device(tokens, cotangent, w_qkv, w_out, row_valid):
@@ -420,8 +421,7 @@
     side = jnp.concatenate([beside, corner], axis=1)
     body = jnp.concatenate([paired[:, HALF:, HALF:], below[:, :, HALF:]], axis=1)
     rolled = jnp.concatenate([side, body], axis=2).reshape(2, LOCAL, D)
-    d_x, terms = window_call(rolled[0], rolled[1], w_qkv, w_out, pair_bias(row_valid))
-    grad_qkv, grad_out = scatter_call(terms)
+    d_x, grad_qkv, grad_out = window_call(rolled[0], rolled[1], w_qkv, w_out, invalid_keys(row_valid))
     d_grid = d_x.reshape(ROWS, COLS, D)
     side = d_grid[:, :HALF]
     from_left = passed_along(side[:-HALF], ("lon",), 1)

time: 160 us -> 138 us (0.86)
  Pallas kernels: 116 us -> 92.4 us
  local copies, waits for them, and re-layouts: 17.8 us -> 12.8 us
  waiting for transfers between devices: 0.02 us -> 4.08 us
  starting transfers between devices: 13.3 us -> 16.4 us
    pallas_call x1 -> x0, Pallas kernels: 47 us -> none  [scatter_call(): pl.pallas_call(scatter_kernel, out_shape=(jax.ShapeDtypeStruct((8, 3 * D)...]
    pallas_call x1, Pallas kernels: 69.5 us -> 92.4 us  [window_call(): pl.pallas_call(window_kernel, out_shape=(jax.ShapeDtypeStruct((LOCAL, D),...]
    gather x4 -> x0, local copies, waits for them, and re-layouts: 4.24 us -> none  [the longest x2 2.13 us: pair_bias(): token_wrap = wrap[:, token_row]]
    ppermute x6, waiting for transfers between devices: 0.02 us -> 4.08 us  [passed_along(): return lax.ppermute(value, axes if len(axes) > 1 else axes[0], pairs)]
    ppermute x6, starting transfers between devices: 13.3 us -> 16.4 us  [passed_along(): return lax.ppermute(value, axes if len(axes) > 1 else axes[0], pairs)]
    select_n x3 -> x0, other arithmetic: 2.43 us -> none  [the longest x1 1.22 us: pair_bias(): return jnp.where(allowed, -SHARP * LOG2E, BLOCKED).astype(F32)]
  transfers between devices with their start and end apart: 6 -> 6, of which waited for: 0 -> 2; matrix products, arithmetic and copies ran while one was open for 11% -> 8% of each run, Pallas kernels for 30% -> 0%
where the time goes in v2:
time: 138 us; the launch traced here: 137 us
  Pallas kernels  92.4 us (67%)
  starting transfers between devices  16.4 us (12%)
  local copies, waits for them, and re-layouts  12.8 us (9%)
  other arithmetic  10.6 us (8%)
  waiting for transfers between devices  4.08 us (3%)
    pallas_call x1, Pallas kernels, window_call(): pl.pallas_call(window_kernel, out_shape=(jax.ShapeDtypeStruct((LOCAL, D),...  92.4 us
    ppermute x6, starting transfers between devices, passed_along(): return lax.ppermute(value, axes if len(axes) > 1 else axes[0], pairs)  16.4 us
    ppermute x6, waiting for transfers between devices, passed_along(): return lax.ppermute(value, axes if len(axes) > 1 else axes[0], pairs)  4.08 us
    concatenate x1, other arithmetic, on_device(): rolled = jnp.concatenate([side, body], axis=2).reshape(2, LOCAL, D)  3.17 us
    another operation x2, other arithmetic, on_device(): paired = jnp.stack([tokens, cotangent])  3.05 us
  transfers between devices with their start and end apart: 6, of which 2 were waited for; matrix products, arithmetic and copies ran while one was open for 8% of the time, Pallas kernels for 0%

profile of v2, /device:TPU:1, one launch (start us, length us, event | category | flops | bytes accessed | tf_op | source)
XLA Modules:
  0.0 137.0 jit_solution(16061304843057631466)
XLA Ops:
  0.6 0.0 copy-start.1
  0.6 0.0 copy-start
  0.7 1.5 %pad_maximum_fusion = bf16[2,33,3,1024]{3,2,1,0:T(4,128)(2,1)S(1)} fusion(bf16[1,36,24,1024]{3,2,1,0:T(8,128)(2,1)} %bitcast.6, bf16[1,36,24,1024]{3,2,1,0:T(8,128)(2,1)} %bitcast.10), kind=kLoop, calls=%fused_computation.5 | loop fusion | flops 811008 | bytes 3944448 | tf_op jit(solution)/shard_map/slice | solution.py:419
  2.2 1.1 copy.8
  3.3 0.0 copy-start.4
  3.3 0.0 slice-start
  3.3 1.4 %collective-permute-start = (bf16[2,33,3,1024]{3,0,2,1:T(2,128)(2,1)}, bf16[2,33,3,1024]{3,0,2,1:T(2,128)(2,1)}, u32[]{:S(2)}, u32[]{:S(2)}) collective-permute-start(bf16[2,33,3,1024]{3,0,2,1:T(2,128)(2,1)} %copy.8), channel_id=1, source_target_pairs={{0,120},{8,0},{16,8},{24,16},{32,24},{40,32},{48,40},{56,48},{64,5... | collective-permute-start | bytes 1216520 | tf_op jit(solution)/shard_map/ppermute | solution.py:408
  4.7 0.0 copy-done.1
  4.7 0.0 copy-done
  4.7 0.8 pad_maximum_fusion.1
  5.5 5.2 %collective-permute-start.2 = (bf16[2,3,24,1024]{3,2,1,0:T(8,128)(2,1)}, bf16[2,3,24,1024]{3,2,1,0:T(8,128)(2,1)}, u32[]{:S(2)}, u32[]{:S(2)}) collective-permute-start(bf16[2,3,24,1024]{3,2,1,0:T(8,128)(2,1)} %pad_maximum_fusion.1), channel_id=1, source_target_pairs={{0,7},{1,0},{2,1},{3,2},{4,3},{5,4},{6,5},{7,6},{8,15},{9,8},{10,9... | collective-permute-start | bytes 884744 | tf_op jit(solution)/shard_map/ppermute | solution.py:408
  10.7 0.6 pad_maximum_fusion.2
  11.3 4.7 %collective-permute-start.1 = (bf16[2,3,3,1024]{3,2,1,0:T(4,128)(2,1)}, bf16[2,3,3,1024]{3,2,1,0:T(4,128)(2,1)}, u32[]{:S(2)}, u32[]{:S(2)}) collective-permute-start(bf16[2,3,3,1024]{3,2,1,0:T(4,128)(2,1)} %pad_maximum_fusion.2), channel_id=1, source_target_pairs={{0,127},{1,120},{2,121},{3,122},{4,123},{5,124},{6,125},{7,126},{8... | collective-permute-start | bytes 110600 | tf_op jit(solution)/shard_map/ppermute | solution.py:408
  16.0 0.0 copy-done.4
  16.0 0.1 slice.59
  16.1 0.0 slice-done
  16.1 0.1 pad_add_fusion
  16.2 2.3 %fusion = bf16[2,33,21,1024]{3,2,1,0:T(8,128)(2,1)} fusion(bf16[1,36,24,1024]{3,2,1,0:T(8,128)(2,1)S(1)} %bitcast.13, bf16[1,36,24,1024]{3,2,1,0:T(8,128)(2,1)S(1)} %bitcast.9), kind=kLoop, calls=%fused_computation.3 | loop fusion | flops 1419264 | bytes 6377472 | tf_op jit(solution)/shard_map/stack | solution.py:417
  18.5 0.1 convert_subtract_fusion
  18.6 0.1 broadcast_in_dim.7
  18.6 0.1 broadcast_in_dim.8
  18.7 0.7 broadcast_in_dim.9.invalid
  19.4 0.0 collective-permute-done.2
  19.4 1.0 slice.69
  20.4 0.0 collective-permute-done
  20.4 1.2 copy.9
  21.7 0.0 collective-permute-done.1
  21.7 3.2 %maximum_maximum_fusion = bf16[2,36,24,1024]{3,2,1,0:T(8,128)(2,1)S(1)} fusion(bf16[2,3,21,1024]{3,2,1,0:T(8,128)(2,1)S(1)} %slice.69, bf16[2,33,21,1024]{3,2,1,0:T(8,128)(2,1)} %fusion, bf16[2,3,3,1024]{3,2,1,0:T(4,128)(2,1)} %collective-permute-done.1, bf16[2,33,3,1024]{3,2,1,0:T(4,128)(2,1)S(1)} %copy.9), kind=kLoop, calls=%fused_computation.2 | loop fusion | flops 14155776 | bytes 7077888 | tf_op jit(solution)/shard_map/concatenate | solution.py:423
  24.8 2.2 %fusion.1 = (bf16[1,36,24,1024]{3,2,1,0:T(8,128)(2,1)}, bf16[1,36,24,1024]{3,2,1,0:T(8,128)(2,1)}) fusion(bf16[2,36,24,1024]{3,2,1,0:T(8,128)(2,1)S(1)} %maximum_maximum_fusion), kind=kLoop, calls=%fused_computation.10 | loop fusion | bytes 7077888 | tf_op jit(solution)/shard_map/slice | solution.py:424
  27.0 92.4 %windows.1 = (bf16[864,1024]{1,0:T(8,128)(2,1)}, f32[8,3072]{1,0:T(8,128)}, f32[8,1024]{1,0:T(8,128)}) custom-call(bf16[864,1024]{1,0:T(8,128)(2,1)} %bitcast.15, bf16[864,1024]{1,0:T(8,128)(2,1)} %bitcast.14, bf16[1024,3072]{1,0:T(8,128)(2,1)} %w_qkv.1, bf16[1024,1024]{1,0:T(8,128)(2,1)} %w_out.1, f32[6,144]{1,0:T(8,128)} %broadcast_in_dim.9.invalid), custom_call_target="tpu_custom_call" | custom-call | tf_op jit(solution)/shard_map/windows/pallas_call | solution.py:232
  119.4 1.1 slice.73
  120.6 1.9 %collective-permute-start.4 = (bf16[33,3,1024]{2,1,0:T(4,128)(2,1)S(1)}, bf16[33,3,1024]{2,1,0:T(4,128)(2,1)S(1)}, u32[]{:S(2)}, u32[]{:S(2)}) collective-permute-start(bf16[33,3,1024]{2,1,0:T(4,128)(2,1)S(1)} %slice.73), channel_id=1, source_target_pairs={{0,8},{8,16},{16,24},{24,32},{32,40},{40,48},{48,56},{56,64},{64,7... | collective-permute-start | bytes 608264 | tf_op jit(solution)/shard_map/ppermute | solution.py:408
  122.5 0.9 slice.63
  123.4 2.5 %collective-permute-start.5 = (bf16[3,24,1024]{2,1,0:T(8,128)(2,1)S(1)}, bf16[3,24,1024]{2,1,0:T(8,128)(2,1)S(1)}, u32[]{:S(2)}, u32[]{:S(2)}) collective-permute-start(bf16[3,24,1024]{2,1,0:T(8,128)(2,1)S(1)} %bitcast.19), channel_id=1, source_target_pairs={{0,1},{1,2},{2,3},{3,4},{4,5},{5,6},{6,7},{7,0},{8,9},{9,10},{10,1... | collective-permute-start | bytes 442376 | tf_op jit(solution)/shard_map/ppermute | solution.py:408
  125.9 0.8 slice.72
  126.7 0.0 copy-start.2
  126.7 0.0 copy-start.3
  126.7 0.7 collective-permute-start.3
  127.4 2.2 %slice.75 = bf16[33,21,1024]{2,1,0:T(8,128)(2,1)S(1)} slice(bf16[36,24,1024]{2,1,0:T(8,128)(2,1)} %bitcast.18), slice={[0:33], [3:24], [0:1024]} | slice | bytes 2838528 | tf_op jit(solution)/shard_map/slice | solution.py:431
  129.5 2.7 %collective-permute-done.5 = bf16[3,24,1024]{2,1,0:T(8,128)(2,1)S(1)} collective-permute-done((bf16[3,24,1024]{2,1,0:T(8,128)(2,1)S(1)}, bf16[3,24,1024]{2,1,0:T(8,128)(2,1)S(1)}, u32[]{:S(2)}, u32[]{:S(2)}) %collective-permute-start.5) | collective-permute-done | bytes 147488 | tf_op jit(solution)/shard_map/ppermute | solution.py:408
  132.3 1.4 %collective-permute-done.3 = bf16[3,3,1024]{2,1,0:T(4,128)(2,1)S(1)} collective-permute-done((bf16[3,3,1024]{2,1,0:T(4,128)(2,1)S(1)}, bf16[3,3,1024]{2,1,0:T(4,128)(2,1)S(1)}, u32[]{:S(2)}, u32[]{:S(2)}) %collective-permute-start.3) | collective-permute-done | bytes 18464 | tf_op jit(solution)/shard_map/ppermute | solution.py:408
  133.7 0.0 collective-permute-done.4
  133.7 2.1 %maximum_maximum_fusion.1 = bf16[36,24,1024]{2,1,0:T(8,128)(2,1)} fusion(bf16[33,21,1024]{2,1,0:T(8,128)(2,1)S(1)} %slice.75, bf16[3,21,1024]{2,1,0:T(8,128)(2,1)S(1)} %slice.74, bf16[33,3,1024]{2,1,0:T(4,128)(2,1)S(1)} %collective-permute-done.4, bf16[3,3,1024]{2,1,0:T(4,128)(2,1)S(1)} %collective-permute-done.3), kind=kLoop, calls=%fused_computation.4 | loop fusion | flops 7077888 | bytes 3538944 | tf_op jit(solution)/shard_map/concatenate | solution.py:432
  135.7 0.0 copy-done.2
  135.7 0.6 copy.12
  136.4 0.0 copy-done.3
  136.4 0.6 copy.13
  (1 shorter events, 0.0 us)
Async XLA Ops:
  0.6 4.1 %copy-start.1 = (bf16[36,24,1024]{2,1,0:T(8,128)(2,1)S(1)}, bf16[36,24,1024]{2,1,0:T(8,128)(2,1)}, u32[]{:S(2)}) copy-start(bf16[36,24,1024]{2,1,0:T(8,128)(2,1)} %param.5) | copy-start | bytes 5308420
  0.6 4.1 %copy-start = (bf16[36,24,1024]{2,1,0:T(8,128)(2,1)S(1)}, bf16[36,24,1024]{2,1,0:T(8,128)(2,1)}, u32[]{:S(2)}) copy-start(bf16[36,24,1024]{2,1,0:T(8,128)(2,1)} %param.6) | copy-start | bytes 5308420
  3.3 12.7 %copy-start.4 = (s32[288]{0:T(512)S(1)}, s32[288]{0:T(512)}, u32[]{:S(2)}) copy-start(s32[288]{0:T(512)} %param.9) | copy-start | bytes 3460
  3.3 12.8 %slice-start = ((s32[288]{0:T(512)}), s32[3]{0:T(128)S(1)}, s32[]{:S(2)}) async-start(s32[288]{0:T(512)} %param.9), calls=%async_computation | async-start | bytes 1024 | tf_op jit(solution)/shard_map/jit(_roll_static)/slice | solution.py:412
  3.3 17.1 %collective-permute-start = (bf16[2,33,3,1024]{3,0,2,1:T(2,128)(2,1)}, bf16[2,33,3,1024]{3,0,2,1:T(2,128)(2,1)}, u32[]{:S(2)}, u32[]{:S(2)}) collective-permute-start(bf16[2,33,3,1024]{3,0,2,1:T(2,128)(2,1)} %copy.8), channel_id=1, source_target_pairs={{0,120},{8,0},{16,8},{24,16},{32,24},{40,32},{48,40},{56,48},{64,5... | collective-permute-start | bytes 1216520 | tf_op jit(solution)/shard_map/ppermute | solution.py:408
  5.5 13.9 %collective-permute-start.2 = (bf16[2,3,24,1024]{3,2,1,0:T(8,128)(2,1)}, bf16[2,3,24,1024]{3,2,1,0:T(8,128)(2,1)}, u32[]{:S(2)}, u32[]{:S(2)}) collective-permute-start(bf16[2,3,24,1024]{3,2,1,0:T(8,128)(2,1)} %pad_maximum_fusion.1), channel_id=1, source_target_pairs={{0,7},{1,0},{2,1},{3,2},{4,3},{5,4},{6,5},{7,6},{8,15},{9,8},{10,9... | collective-permute-start | bytes 884744 | tf_op jit(solution)/shard_map/ppermute | solution.py:408
  11.3 10.3 %collective-permute-start.1 = (bf16[2,3,3,1024]{3,2,1,0:T(4,128)(2,1)}, bf16[2,3,3,1024]{3,2,1,0:T(4,128)(2,1)}, u32[]{:S(2)}, u32[]{:S(2)}) collective-permute-start(bf16[2,3,3,1024]{3,2,1,0:T(4,128)(2,1)} %pad_maximum_fusion.2), channel_id=1, source_target_pairs={{0,127},{1,120},{2,121},{3,122},{4,123},{5,124},{6,125},{7,126},{8... | collective-permute-start | bytes 110600 | tf_op jit(solution)/shard_map/ppermute | solution.py:408
  120.6 13.1 %collective-permute-start.4 = (bf16[33,3,1024]{2,1,0:T(4,128)(2,1)S(1)}, bf16[33,3,1024]{2,1,0:T(4,128)(2,1)S(1)}, u32[]{:S(2)}, u32[]{:S(2)}) collective-permute-start(bf16[33,3,1024]{2,1,0:T(4,128)(2,1)S(1)} %slice.73), channel_id=1, source_target_pairs={{0,8},{8,16},{16,24},{24,32},{32,40},{40,48},{48,56},{56,64},{64,7... | collective-permute-start | bytes 608264 | tf_op jit(solution)/shard_map/ppermute | solution.py:408
  123.4 8.8 %collective-permute-start.5 = (bf16[3,24,1024]{2,1,0:T(8,128)(2,1)S(1)}, bf16[3,24,1024]{2,1,0:T(8,128)(2,1)S(1)}, u32[]{:S(2)}, u32[]{:S(2)}) collective-permute-start(bf16[3,24,1024]{2,1,0:T(8,128)(2,1)S(1)} %bitcast.19), channel_id=1, source_target_pairs={{0,1},{1,2},{2,3},{3,4},{4,5},{5,6},{6,7},{7,0},{8,9},{9,10},{10,1... | collective-permute-start | bytes 442376 | tf_op jit(solution)/shard_map/ppermute | solution.py:408
  126.7 9.0 %copy-start.2 = (f32[8,3072]{1,0:T(8,128)S(1)}, f32[8,3072]{1,0:T(8,128)}, u32[]{:S(2)}) copy-start(f32[8,3072]{1,0:T(8,128)} %get-tuple-element.15) | copy-start | bytes 294916
  126.7 9.7 %copy-start.3 = (f32[8,1024]{1,0:T(8,128)S(1)}, f32[8,1024]{1,0:T(8,128)}, u32[]{:S(2)}) copy-start(f32[8,1024]{1,0:T(8,128)} %get-tuple-element.16) | copy-start | bytes 98308
  126.7 6.9 %collective-permute-start.3 = (bf16[3,3,1024]{2,1,0:T(4,128)(2,1)S(1)}, bf16[3,3,1024]{2,1,0:T(4,128)(2,1)S(1)}, u32[]{:S(2)}, u32[]{:S(2)}) collective-permute-start(bf16[3,3,1024]{2,1,0:T(4,128)(2,1)S(1)} %slice.72), channel_id=1, source_target_pairs={{0,9},{1,10},{2,11},{3,12},{4,13},{5,14},{6,15},{7,8},{8,17},{9,18... | collective-permute-start | bytes 55304 | tf_op jit(solution)/shard_map/ppermute | solution.py:408

commit v3 on v2

--- a/solution.py
+++ b/solution.py
@@ -1,4 +1,3 @@
-import functools
 import math
 
 import jax
@@ -22,6 +21,9 @@
 CHUNKS = D // GROUP
 GROUP_HEADS = GROUP // HEAD_DIM
 STACK = GROUP_HEADS * STRIP
+EDGE = 112
+EDGES = 128
+BAND = 80
 
 SHARP = 10.0
 LOG2E = math.log2(math.e)
@@ -60,10 +62,33 @@
     return out
 
 
-def prologue(x, cot, normed, normed_t, cot_t, inv_rms):
+def shift_rows(ext, s):
+    return ext[pl.ds(pl.multiple_of(s * STRIP + 64, 16), STRIP + 16), :].astype(F32)[8 : 8 + STRIP]
+
+
+def edge_pick():
+    at = lax.broadcasted_iota(jnp.int32, (EDGE, LOCAL), 0)
+    token = lax.broadcasted_iota(jnp.int32, (EDGE, LOCAL), 1)
+    return jnp.where(token == at // HALF * COLS + at % HALF, 1.0, 0.0).astype(BF16)
+
+
+def edge_spread(s, near, far):
+    token = lax.broadcasted_iota(jnp.int32, (STRIP, EDGES), 0)
+    at = lax.broadcasted_iota(jnp.int32, (STRIP, EDGES), 1)
+    row, col = s * WIN + token // COLS, token % COLS
+    source = jnp.where(near(row), far[0] + HALF * row + col, far[1] + HALF * row + col)
+    return jnp.where((col < HALF) & (at == source), 1.0, 0.0).astype(BF16)
+
+
+def prologue(x_ext, cot_ext, edges, x, cot, normed, normed_t, cot_t, inv_rms):
+    is_edge = lax.broadcasted_iota(jnp.int32, (STRIP, 1), 0) % COLS < HALF
+
     def norm_strip(s, _):
         rows = pl.ds(pl.multiple_of(s * STRIP, 16), STRIP)
-        xf = x[rows, :].astype(F32)
+        spread = edge_spread(s, lambda row: row < ROWS - HALF, (HALF * HALF, EDGE - HALF * (ROWS - HALF)))
+        cot[rows, :] = jnp.where(is_edge, dot(spread, edges[1]), shift_rows(cot_ext, s)).astype(BF16)
+        xf = jnp.where(is_edge, dot(spread, edges[0]), shift_rows(x_ext, s))
+        x[rows, :] = xf.astype(BF16)
         inv = lax.rsqrt(jnp.mean(xf * xf, axis=-1, keepdims=True) + EPSILON)
         inv_rms[rows, :] = inv
         normed[rows, :] = (xf * inv).astype(BF16)
@@ -156,45 +181,105 @@
     d_normed[:, cols] = dot(d_qkv[...], w_qkv[cols, :], NT)
 
 
-def token_grad(x, inv_rms, d_normed, d_x):
+def token_grad(x, inv_rms, d_normed, d_ext):
     def strip(s, _):
         rows = pl.ds(pl.multiple_of(s * STRIP, 16), STRIP)
         xf = x[rows, :].astype(F32)
         dn = d_normed[rows, :]
         inv = inv_rms[rows, :]
         pull = jnp.mean(dn * xf, axis=-1, keepdims=True) * (inv * inv * inv)
-        d_x[rows, :] = (inv * dn - xf * pull).astype(BF16)
+        d_ext[pl.ds(pl.multiple_of(s * STRIP + BAND, 16), STRIP), :] = (inv * dn - xf * pull).astype(BF16)
         return 0
 
     lax.fori_loop(0, STRIPS, strip, 0)
 
 
-def pair_bias(invalid, bias):
+def assemble(d_ext, d_edges, d_tokens):
+    is_edge = lax.broadcasted_iota(jnp.int32, (STRIP, 1), 0) % COLS < HALF
+
+    def strip(s, _):
+        start = pl.multiple_of(s * STRIP, 16)
+        own = d_ext[pl.ds(start, STRIP + 16), :].astype(F32)[8 : 8 + STRIP]
+        spread = edge_spread(s, lambda row: row >= HALF, (-HALF * HALF, EDGE + HALF))
+        d_tokens[pl.ds(start, STRIP), :] = jnp.where(is_edge, dot(spread, d_edges[...]), own).astype(BF16)
+        return 0
+
+    lax.fori_loop(0, STRIPS, strip, 0)
+
+
+def pair_bias(row_valid, bias):
     query = lax.broadcasted_iota(jnp.int32, (STRIP, STRIP), 0)
     key = lax.broadcasted_iota(jnp.int32, (STRIP, STRIP), 1)
     window = lambda t: (t % COLS + COLS - HALF) % COLS // WIN
     half = lambda t: t // (HALF * COLS)
     same_window = window(query) == window(key)
     same_half = half(query) == half(key)
-    seam = lax.axis_index("lat") == lax.axis_size("lat") - 1
+    lat, bands = lax.axis_index("lat"), lax.axis_size("lat")
     open_bias = jnp.where(same_window, -SHARP * LOG2E, BLOCKED)
     seam_bias = jnp.where(same_window & same_half, -SHARP * LOG2E, BLOCKED)
     others = jnp.where(query == key, 0.0, BLOCKED)
+    key_row = lax.broadcasted_iota(jnp.int32, (1, STRIP), 1) // COLS
     for s in range(STRIPS):
-        base = open_bias if s < STRIPS - 1 else jnp.where(seam, seam_bias, open_bias)
-        bias[s] = base + others * invalid[s : s + 1, :]
+        base = open_bias if s < STRIPS - 1 else jnp.where(lat == bands - 1, seam_bias, open_bias)
+        invalid = jnp.zeros((1, STRIP), F32)
+        for i in range(WIN):
+            flag = 1.0 - row_valid[(lat * ROWS + s * WIN + i + HALF) % (ROWS * bands)].astype(F32)
+            invalid = jnp.where(key_row == i, flag, invalid)
+        bias[s] = base + others * invalid
+
+
+def neighbour(lat_step, lon_step):
+    lon, lons = lax.axis_index("lon"), lax.axis_size("lon")
+    lat, lats = lax.axis_index("lat"), lax.axis_size("lat")
+    return {"lon": (lon + lon_step + lons) % lons, "lat": (lat + lat_step + lats) % lats}
+
+
+def remote(source, target, send, recv, slot, peer):
+    return pltpu.make_async_remote_copy(
+        src_ref=source, dst_ref=target, send_sem=send.at[slot], recv_sem=recv.at[slot], device_id=peer, device_id_type=MESH
+    )
 
 
 def window_kernel(
-    x, cot, w_qkv, w_out, invalid, d_x, grad_qkv, grad_out,
-    bias, normed, normed_t, cot_t, inv_rms, qb, kb, vb, dab, ob, d_qkv, d_normed, terms,
-    got_0, sum_0, got_1, sum_1, got_2, sum_2, got_3, sum_3, send, recv,
+    tokens, cotangent, w_qkv_hbm, w_out_hbm, row_valid, d_tokens, grad_qkv, grad_out,
+    x_ext, cot_ext, w_qkv, w_out, edge_out, edges, d_ext, d_edge_out, d_edges,
+    bias, x, cot, normed, normed_t, cot_t, inv_rms, qb, kb, vb, dab, ob, d_qkv, d_normed, terms,
+    got_0, got_1, sum_1, got_2, sum_2, got_3, sum_3, send, recv, halo_send, halo_recv, load,
 ):
     greet()
-    pair_bias(invalid, bias)
-    prologue(x, cot, normed, normed_t, cot_t, inv_rms)
-    first = lambda p: rs_first(p, terms, got_0, sum_0, got_1, send, recv)
-    second = lambda p: rs_next(p, 0, sum_0, got_1, sum_1, got_2, send, recv)
+    loads = [
+        pltpu.make_async_copy(tokens, x_ext.at[0:LOCAL], load.at[0]),
+        pltpu.make_async_copy(cotangent, cot_ext.at[0:LOCAL], load.at[1]),
+        pltpu.make_async_copy(w_qkv_hbm, w_qkv, load.at[2]),
+        pltpu.make_async_copy(w_out_hbm, w_out, load.at[3]),
+    ]
+    for copy in loads:
+        copy.start()
+    pair_bias(row_valid, bias)
+    pick = edge_pick()
+    for copy in loads[:2]:
+        copy.wait()
+    met()
+    up, left, corner = neighbour(-1, 0), neighbour(0, -1), neighbour(-1, -1)
+    halos = [
+        remote(x_ext.at[0:BAND], x_ext.at[LOCAL : LOCAL + BAND], halo_send, halo_recv, 0, up),
+        remote(cot_ext.at[0:BAND], cot_ext.at[LOCAL : LOCAL + BAND], halo_send, halo_recv, 1, up),
+        remote(edge_out, edges.at[:, 0:EDGE], halo_send, halo_recv, 2, left),
+        remote(edge_out.at[:, 0:16], edges.at[:, EDGE:EDGES], halo_send, halo_recv, 3, corner),
+    ]
+    halos[0].start()
+    halos[1].start()
+    edge_out[0] = dot(pick, x_ext[0:LOCAL, :]).astype(BF16)
+    edge_out[1] = dot(pick, cot_ext[0:LOCAL, :]).astype(BF16)
+    halos[2].start()
+    halos[3].start()
+    for copy in halos:
+        copy.wait_recv()
+    prologue(x_ext, cot_ext, edges, x, cot, normed, normed_t, cot_t, inv_rms)
+    for copy in loads[2:]:
+        copy.wait()
+    first = lambda p: rs_first(p, terms, got_0, got_1, send, recv)
+    second = lambda p: rs_next(p, 0, terms, got_1, sum_1, got_2, send, recv)
     third = lambda p: rs_next(p, 1, sum_1, got_2, sum_2, got_3, send, recv)
     last = lambda p: rs_next(p, 2, sum_2, got_3, sum_3, None, send, recv)
 
@@ -202,10 +287,10 @@
         project(p, cot, w_qkv, w_out, normed, qb, kb, vb, dab)
         pl.when(p > 0)(lambda: first(p - 1))
         attend(p, bias, qb, kb, vb, dab, ob, d_qkv)
-        pl.when(p > 0)(lambda: second(p - 1))
+        pl.when(p > 1)(lambda: third(p - 2))
         weight_terms(p, normed_t, cot_t, d_qkv, ob, terms)
         rs_start(p, terms, got_0, send, recv)
-        pl.when(p > 0)(lambda: third(p - 1))
+        pl.when(p > 0)(lambda: second(p - 1))
         return 0
 
     lax.fori_loop(0, CHUNKS, chunk, 0)
@@ -213,22 +298,39 @@
     def tail(n, _):
         normed_grad(n, w_qkv, d_qkv, d_normed)
         pl.when(n == 0)(lambda: first(CHUNKS - 1))
-        pl.when(n == 3)(lambda: second(CHUNKS - 1))
+        pl.when(n == 1)(lambda: third(CHUNKS - 2))
         return 0
 
     lax.fori_loop(0, D // 256, tail, 0)
-    token_grad(x, inv_rms, d_normed, d_x)
+    token_grad(x, inv_rms, d_normed, d_ext)
+    down, right, far_corner = neighbour(1, 0), neighbour(0, 1), neighbour(1, 1)
+    returns = [
+        remote(d_ext.at[LOCAL : LOCAL + BAND], d_ext.at[0:BAND], halo_send, halo_recv, 4, down),
+        remote(d_edge_out, d_edges.at[0:EDGE], halo_send, halo_recv, 5, right),
+        remote(d_edge_out.at[EDGE - 16 : EDGE], d_edges.at[EDGE:EDGES], halo_send, halo_recv, 6, far_corner),
+    ]
+    returns[0].start()
+    d_edge_out[...] = dot(edge_pick(), d_ext[BAND : BAND + LOCAL, :]).astype(BF16)
+    returns[1].start()
+    returns[2].start()
+    second(CHUNKS - 1)
+    for copy in returns:
+        copy.wait_recv()
+    assemble(d_ext, d_edges, d_tokens)
     third(CHUNKS - 1)
     lax.fori_loop(0, CHUNKS, lambda p, _: (last(p), 0)[1], 0)
     write_grads(sum_3, grad_qkv, grad_out)
-    rs_finish(terms, got_0, (sum_0, sum_1, sum_2), (got_1, got_2, got_3), send, recv)
+    rs_finish(terms, got_0, (terms, sum_1, sum_2), (got_1, got_2, got_3), send, recv)
+    for copy in halos + returns:
+        copy.wait_send()
 
 
 TERMS = (CHUNKS, 2, 2, 4, 4, 4, 16, GROUP)
 
 
-def window_call(x, cot, w_qkv, w_out, invalid):
+def window_call(tokens, cotangent, w_qkv, w_out, row_valid):
     vmem = pl.BlockSpec(memory_space=pltpu.VMEM)
+    anywhere = pl.BlockSpec(memory_space=pl.ANY)
     return pl.pallas_call(
         window_kernel,
         out_shape=(
@@ -236,10 +338,21 @@
             jax.ShapeDtypeStruct((8, 3 * D), F32),
             jax.ShapeDtypeStruct((8, D), F32),
         ),
-        in_specs=[vmem] * 5,
+        in_specs=[anywhere] * 4 + [pl.BlockSpec(memory_space=pltpu.SMEM)],
         out_specs=(vmem, vmem, vmem),
         scratch_shapes=[
+            pltpu.VMEM((LOCAL + BAND, D), BF16),
+            pltpu.VMEM((LOCAL + BAND, D), BF16),
+            pltpu.VMEM((D, 3 * D), BF16),
+            pltpu.VMEM((D, D), BF16),
+            pltpu.VMEM((2, EDGE, D), BF16),
+            pltpu.VMEM((2, EDGES, D), BF16),
+            pltpu.VMEM((BAND + LOCAL, D), BF16),
+            pltpu.VMEM((EDGE, D), BF16),
+            pltpu.VMEM((EDGES, D), BF16),
             pltpu.VMEM((STRIPS, STRIP, STRIP), F32),
+            pltpu.VMEM((LOCAL, D), BF16),
+            pltpu.VMEM((LOCAL, D), BF16),
             pltpu.VMEM((LOCAL, D), BF16),
             pltpu.VMEM((D, LOCAL), BF16),
             pltpu.VMEM((D, LOCAL), BF16),
@@ -253,12 +366,13 @@
             pltpu.VMEM((LOCAL, D), F32),
             pltpu.VMEM(TERMS, BF16),
         ]
-        + scatter_scratch(),
+        + scatter_scratch()
+        + [pltpu.SemaphoreType.DMA((7,)), pltpu.SemaphoreType.DMA((7,)), pltpu.SemaphoreType.DMA((4,))],
         compiler_params=pltpu.CompilerParams(
-            collective_id=0, has_side_effects=True, vmem_limit_bytes=60 * 1024 * 1024
+            collective_id=0, has_side_effects=True, vmem_limit_bytes=62 * 1024 * 1024
         ),
         name="windows",
-    )(x, cot, w_qkv, w_out, invalid)
+    )(tokens, cotangent, w_qkv, w_out, row_valid)
 
 
 def place():
@@ -287,15 +401,20 @@
 ORDERS = (("x", "y", "z"), ("z", "y", "x"))
 
 
+AROUND = ((-1, 0), (0, -1), (-1, -1), (1, 0), (0, 1), (1, 1))
+
+
 def greet():
     x, y, z, core = place()
-    barrier = pltpu.get_barrier_semaphore()
-    pl.semaphore_signal(barrier, inc=1, device_id=device(x, y, z, 1 - core), device_id_type=MESH)
-    for axis in "xyz":
-        for step in (1, 2, 3):
-            _, peer = axis_peer(axis, step)
-            pl.semaphore_signal(barrier, inc=1, device_id=peer, device_id_type=MESH)
-    pl.semaphore_wait(barrier, 10)
+    peers = [device(x, y, z, 1 - core)]
+    peers += [axis_peer(axis, step)[1] for axis in "xyz" for step in (1, 2, 3)]
+    peers += [neighbour(*step) for step in AROUND]
+    for peer in peers:
+        pl.semaphore_signal(pltpu.get_barrier_semaphore(), inc=1, device_id=peer, device_id_type=MESH)
+
+
+def met():
+    pl.semaphore_wait(pltpu.get_barrier_semaphore(), 10 + len(AROUND))
 
 
 def core_copy(p, terms, got_0, send, recv):
@@ -314,7 +433,7 @@
     at, peer = axis_peer(ORDERS[half][stage], step)
     slot = 3 * half + step - 1
     return pltpu.make_async_remote_copy(
-        src_ref=source.at[p, half, at],
+        src_ref=source.at[p, place()[3], half, at] if stage == 0 else source.at[p, half, at],
         dst_ref=target.at[p, half, step - 1],
         send_sem=send.at[p, 1 + stage, slot],
         recv_sem=recv.at[p, 1 + stage, slot],
@@ -335,21 +454,22 @@
     core_copy(p, terms, got_0, send, recv).start()
 
 
-def rs_first(p, terms, got_0, sum_0, got_1, send, recv):
+def rs_first(p, terms, got_0, got_1, send, recv):
     core = place()[3]
     core_copy(p, terms, got_0, send, recv).wait_recv()
     for half in (0, 1):
         for a in range(4):
-            sum_0[p, half, a] = terms[p, core, half, a] + got_0[p, half, a]
+            terms[p, core, half, a] = terms[p, core, half, a] + got_0[p, half, a]
     for half, step in STEPS:
-        stage_copy(p, 0, half, step, sum_0, got_1, send, recv).start()
+        stage_copy(p, 0, half, step, terms, got_1, send, recv).start()
 
 
 def rs_next(p, stage, source, got, total, after, send, recv):
     for half, step in STEPS:
         stage_copy(p, stage, half, step, source, got, send, recv).wait_recv()
     for half in (0, 1):
-        mine = source[p, half, my_index(stage, half)].astype(F32)
+        index = (half, my_index(stage, half))
+        mine = source[(p, place()[3]) + index if stage == 0 else (p,) + index].astype(F32)
         for i in range(3):
             mine = mine + got[p, half, i].astype(F32)
         total[p, half] = mine.astype(total.dtype)
@@ -382,7 +502,6 @@
 def scatter_scratch():
     unit = (16, GROUP)
     return [
-        pltpu.VMEM((CHUNKS, 2, 4, 4, 4) + unit, BF16),
         pltpu.VMEM((CHUNKS, 2, 4, 4, 4) + unit, BF16),
         pltpu.VMEM((CHUNKS, 2, 3, 4, 4) + unit, BF16),
         pltpu.VMEM((CHUNKS, 2, 4, 4) + unit, BF16),
@@ -395,42 +514,10 @@
     ]
 
 
-def passed_along(value, axes, steps):
-    sizes = [lax.axis_size(axis) for axis in axes]
-    total = math.prod(sizes)
-    pairs = []
-    for source in range(total):
-        if len(axes) == 1:
-            pairs.append((source, (source + steps) % total))
-        else:
-            first, second = source // sizes[1], source % sizes[1]
-            pairs.append((source, (first + steps) % sizes[0] * sizes[1] + (second + steps) % sizes[1]))
-    return lax.ppermute(value, axes if len(axes) > 1 else axes[0], pairs)
-
-
-def invalid_keys(row_valid):
-    rows = lax.dynamic_slice_in_dim(jnp.roll(row_valid, -HALF), lax.axis_index("lat") * ROWS, ROWS)
-    return jnp.repeat(1.0 - rows.astype(F32), COLS).reshape(STRIPS, STRIP)
-
-
 def on_device(tokens, cotangent, w_qkv, w_out, row_valid):
-    paired = jnp.stack([tokens, cotangent])
-    below = passed_along(paired[:, :HALF], ("lat",), -1)
-    beside = passed_along(paired[:, HALF:, :HALF], ("lon",), -1)
-    corner = passed_along(paired[:, :HALF, :HALF], ("lon", "lat"), -1)
-    side = jnp.concatenate([beside, corner], axis=1)
-    body = jnp.concatenate([paired[:, HALF:, HALF:], below[:, :, HALF:]], axis=1)
-    rolled = jnp.concatenate([side, body], axis=2).reshape(2, LOCAL, D)
-    d_x, grad_qkv, grad_out = window_call(rolled[0], rolled[1], w_qkv, w_out, invalid_keys(row_valid))
-    d_grid = d_x.reshape(ROWS, COLS, D)
-    side = d_grid[:, :HALF]
-    from_left = passed_along(side[:-HALF], ("lon",), 1)
-    from_above = passed_along(d_grid[-HALF:], ("lat",), 1)
-    from_corner = passed_along(side[-HALF:], ("lon", "lat"), 1)
-    side = jnp.concatenate([from_corner, from_left], axis=0)
-    body = jnp.concatenate([from_above[:, HALF:], d_grid[:-HALF, HALF:]], axis=0)
-    d_tokens = jnp.concatenate([side, body], axis=1)
-    return (d_tokens, grad_qkv, grad_out)
+    flat = (LOCAL, D)
+    d_tokens, grad_qkv, grad_out = window_call(tokens.reshape(flat), cotangent.reshape(flat), w_qkv, w_out, row_valid)
+    return (d_tokens.reshape(tokens.shape), grad_qkv, grad_out)
 
 
 def solution(mesh):

time: 138 us -> 113 us (0.82)
  starting transfers between devices: 16.4 us -> 0 us
  Pallas kernels: 92.4 us -> 108 us
  other arithmetic: 10.6 us -> 0 us
  local copies, waits for them, and re-layouts: 12.8 us -> 4.12 us
  waiting for transfers between devices: 4.08 us -> 0 us
    ppermute x6 -> x0, starting transfers between devices: 16.4 us -> none  [passed_along(): return lax.ppermute(value, axes if len(axes) > 1 else axes[0], pairs)]
    pallas_call x1, Pallas kernels: 92.4 us -> 108 us  [window_call(): pl.pallas_call(window_kernel, out_shape=(jax.ShapeDtypeStruct((LOCAL, D),...]
    slice x11 -> x0, local copies, waits for them, and re-layouts: 9.46 us -> none  [the longest x1 2.2 us: on_device(): rolled[1]]
    concatenate x3 -> x0, other arithmetic: 5.3 us -> none  [the longest x1 3.17 us: on_device(): rolled = jnp.concatenate([side, body], axis=2).reshape(2, LOCAL, D)]
    ppermute x6 -> x0, waiting for transfers between devices: 4.08 us -> none  [passed_along(): return lax.ppermute(value, axes if len(axes) > 1 else axes[0], pairs)]
    another operation x2 -> x0, other arithmetic: 3.05 us -> none  [on_device(): paired = jnp.stack([tokens, cotangent])]
    unnamed x12 -> x7, local copies, waits for them, and re-layouts: 1.28 us -> 4.12 us
    slice x2 -> x0, other arithmetic: 2.18 us -> none  [the longest x1 1.55 us: on_device(): beside = passed_along(paired[:, HALF:, :HALF], ('lon',), -1)]
  transfers between devices with their start and end apart: 6 -> 0, of which waited for: 2 -> 0; matrix products, arithmetic and copies ran while one was open for 8% -> 0% of each run, Pallas kernels for 0% -> 0%
where the time goes in v3:
time: 113 us
  Pallas kernels  108 us (96%)
  local copies, waits for them, and re-layouts  4.12 us (4%)
    pallas_call x1, Pallas kernels, window_call(): pl.pallas_call(window_kernel, out_shape=(jax.ShapeDtypeStruct((LOCAL, D),...  108 us
    unnamed x7, local copies, waits for them, and re-layouts  4.12 us

profile of v3, /device:TPU:1, one launch (start us, length us, event | category | flops | bytes accessed | tf_op | source)
XLA Modules:
  0.0 113.0 jit_solution(1325868348719596480)
XLA Ops:
  0.6 108.2 %windows.1 = (bf16[864,1024]{1,0:T(8,128)(2,1)}, f32[8,3072]{1,0:T(8,128)}, f32[8,1024]{1,0:T(8,128)}) custom-call(bf16[864,1024]{1,0:T(8,128)(2,1)} %bitcast.3, bf16[864,1024]{1,0:T(8,128)(2,1)} %bitcast.4, bf16[1024,3072]{1,0:T(8,128)(2,1)} %w_qkv_hbm.1, bf16[1024,1024]{1,0:T(8,128)(2,1)} %w_out_hbm.1, s32[288]{0:T(512)} %row_valid.1), custom_call_target="tpu_custom_call" | custom-call | tf_op jit(solution)/shard_map/windows/pallas_call | solution.py:334
  108.9 0.0 copy-start
  108.9 0.0 copy-start.1
  108.9 2.9 %copy.11 = bf16[36,24,1024]{2,1,0:T(8,128)(2,1)} copy(bf16[36,24,1024]{2,1,0:T(8,128)(2,1)} %bitcast.5) | data formatting | bytes 3538944
  111.7 0.0 copy-done
  111.7 0.6 copy.12
  112.4 0.0 copy-done.1
  112.4 0.6 copy.13
Async XLA Ops:
  108.9 2.9 %copy-start = (f32[8,3072]{1,0:T(8,128)S(1)}, f32[8,3072]{1,0:T(8,128)}, u32[]{:S(2)}) copy-start(f32[8,3072]{1,0:T(8,128)} %get-tuple-element.13) | copy-start | bytes 294916
  108.9 3.5 %copy-start.1 = (f32[8,1024]{1,0:T(8,128)S(1)}, f32[8,1024]{1,0:T(8,128)}, u32[]{:S(2)}) copy-start(f32[8,1024]{1,0:T(8,128)} %get-tuple-element.14) | copy-start | bytes 98308

commit v4 on v3

--- a/solution.py
+++ b/solution.py
@@ -24,6 +24,7 @@
 EDGE = 112
 EDGES = 128
 BAND = 80
+EARLY = STRIP * (STRIPS - 1)
 
 SHARP = 10.0
 LOG2E = math.log2(math.e)
@@ -42,10 +43,9 @@
     return lax.dot_general(a, b, dims, preferred_element_type=F32)
 
 
-def head_sums(t, ones):
-    hi = t.astype(BF16)
-    lo = (t - hi.astype(F32)).astype(BF16)
-    return dot(hi, ones) + dot(lo, ones)
+def head_sums(a, b, ones):
+    both = dot(jnp.concatenate([a, b], axis=0), ones)
+    return both[:STRIP], both[STRIP:]
 
 
 def by_head(t):
@@ -80,7 +80,7 @@
     return jnp.where((col < HALF) & (at == source), 1.0, 0.0).astype(BF16)
 
 
-def prologue(x_ext, cot_ext, edges, x, cot, normed, normed_t, cot_t, inv_rms):
+def normalize(strips, x_ext, cot_ext, edges, x, cot, normed, inv_rms):
     is_edge = lax.broadcasted_iota(jnp.int32, (STRIP, 1), 0) % COLS < HALF
 
     def norm_strip(s, _):
@@ -94,28 +94,28 @@
         normed[rows, :] = (xf * inv).astype(BF16)
         return 0
 
-    lax.fori_loop(0, STRIPS, norm_strip, 0)
-    for at in range(0, LOCAL, 128):
-        width = min(128, LOCAL - at)
-        normed_t[:, at : at + width] = normed[at : at + width, :].T
-        cot_t[:, at : at + width] = cot[at : at + width, :].T
-
-
-def project(p, cot, w_qkv, w_out, normed, qb, kb, vb, dab):
-    def part(i, _):
-        rows = pl.ds(pl.multiple_of(i * 432, 16), 432)
-        base = pl.multiple_of(p * GROUP, GROUP)
-        n = normed[rows, :]
-        qb[rows, :] = dot(n, w_qkv[:, pl.ds(base, GROUP)]).astype(BF16)
-        kb[rows, :] = dot(n, w_qkv[:, pl.ds(base + D, GROUP)]).astype(BF16)
-        vb[rows, :] = dot(n, w_qkv[:, pl.ds(base + 2 * D, GROUP)]).astype(BF16)
-        dab[rows, :] = dot(cot[rows, :], w_out[pl.ds(base, GROUP), :], NT).astype(BF16)
-        return 0
-
-    lax.fori_loop(0, 2, part, 0)
-
-
-def attend(p, bias, qb, kb, vb, dab, ob, d_qkv):
+    lax.fori_loop(*strips, norm_strip, 0)
+
+
+def turn(blocks, cot, normed, normed_t, cot_t):
+    for block in blocks:
+        at = block * 128
+        end = min(at + 128, LOCAL)
+        normed_t[:, at:end] = normed[at:end, :].T
+        cot_t[:, at:end] = cot[at:end, :].T
+
+
+def project(p, start, size, cot, w_qkv, w_out, normed, qb, kb, vb, dab):
+    rows = pl.ds(start, size)
+    base = pl.multiple_of(p * GROUP, GROUP)
+    n = normed[rows, :]
+    qb[rows, :] = dot(n, w_qkv[:, pl.ds(base, GROUP)]).astype(BF16)
+    kb[rows, :] = dot(n, w_qkv[:, pl.ds(base + D, GROUP)]).astype(BF16)
+    vb[rows, :] = dot(n, w_qkv[:, pl.ds(base + 2 * D, GROUP)]).astype(BF16)
+    dab[rows, :] = dot(cot[rows, :], w_out[pl.ds(base, GROUP), :], NT).astype(BF16)
+
+
+def attend(p, strips, bias, qb, kb, vb, dab, ob, d_qkv):
     row_head = lax.broadcasted_iota(jnp.int32, (GROUP, GROUP), 0) // HEAD_DIM
     col_head = lax.broadcasted_iota(jnp.int32, (GROUP, GROUP), 1) // HEAD_DIM
     ones = jnp.where(row_head == col_head, 1.0, 0.0).astype(BF16)
@@ -123,10 +123,10 @@
     def strip(s, _):
         rows = pl.ds(pl.multiple_of(s * STRIP, 16), STRIP)
         base = pl.multiple_of(p * GROUP, GROUP)
-        q = qb[rows, :].astype(F32)
-        k = kb[rows, :].astype(F32)
-        inv_q = lax.rsqrt(head_sums(q * q, ones) + EPSILON)
-        inv_k = lax.rsqrt(head_sums(k * k, ones) + EPSILON)
+        q, k = qb[rows, :], kb[rows, :]
+        q_squares, k_squares = head_sums(q * q, k * k, ones)
+        inv_q = lax.rsqrt(q_squares + EPSILON)
+        inv_k = lax.rsqrt(k_squares + EPSILON)
         q_unit = q * inv_q
         k_unit = k * inv_k
         q_heads = by_head(q_unit.astype(BF16))
@@ -145,43 +145,44 @@
         d_qkv[rows, pl.ds(base + 2 * D, GROUP)] = dot(prob_round, da_heads, TN).astype(BF16)
         dq_unit = SHARP * pick_heads(dot(ds_round, k_round))
         dk_unit = SHARP * dot(ds_round, q_heads, TN)
-        d_q = inv_q * (dq_unit - q_unit * head_sums(q_unit * dq_unit, ones))
-        d_k = inv_k * (dk_unit - k_unit * head_sums(k_unit * dk_unit, ones))
+        q_along, k_along = head_sums((q_unit * dq_unit).astype(BF16), (k_unit * dk_unit).astype(BF16), ones)
+        d_q = inv_q * (dq_unit - q_unit * q_along)
+        d_k = inv_k * (dk_unit - k_unit * k_along)
         d_qkv[rows, pl.ds(base, GROUP)] = d_q.astype(BF16)
         d_qkv[rows, pl.ds(base + D, GROUP)] = d_k.astype(BF16)
         return 0
 
-    lax.fori_loop(0, STRIPS, strip, 0)
-
-
-def weight_terms(p, normed_t, cot_t, d_qkv, ob, terms):
+    lax.fori_loop(*strips, strip, 0, unroll=strips[1] - strips[0])
+
+
+def weight_terms(p, half, normed_t, cot_t, d_qkv, ob, terms):
     def plane(z, _):
         rows = pl.ds(pl.multiple_of(z * 256, 256), 256)
         base = pl.multiple_of(p * GROUP, GROUP)
         n = normed_t[rows, :]
-        g_q = dot(n, d_qkv[:, pl.ds(base, GROUP)])
-        g_k = dot(n, d_qkv[:, pl.ds(base + D, GROUP)])
-        g_v = dot(n, d_qkv[:, pl.ds(base + 2 * D, GROUP)])
-        g_o = dot(cot_t[rows, :], ob[...])
+        if half == 0:
+            upper = dot(n, d_qkv[:, pl.ds(base, GROUP)])
+            lower = dot(n, d_qkv[:, pl.ds(base + D, GROUP)])
+        else:
+            upper = dot(n, d_qkv[:, pl.ds(base + 2 * D, GROUP)])
+            lower = dot(cot_t[rows, :], ob[...])
         for unit in range(32):
             y_lo, core, x, y_hi = unit // 16, unit // 8 % 2, unit // 2 % 4, unit % 2
             y = y_hi * 2 + y_lo
             part = slice(unit * 8, unit * 8 + 8)
-            first = jnp.concatenate([g_q[part], g_k[part]], axis=0)
-            second = jnp.concatenate([g_v[part], g_o[part]], axis=0)
-            terms[p, core, 0, x, y, z] = first.astype(BF16)
-            terms[p, core, 1, z, y, x] = second.astype(BF16)
+            both = jnp.concatenate([upper[part], lower[part]], axis=0).astype(BF16)
+            terms[(p, core, half) + ((x, y, z) if half == 0 else (z, y, x))] = both
         return 0
 
     lax.fori_loop(0, 4, plane, 0)
 
 
-def normed_grad(n, w_qkv, d_qkv, d_normed):
+def normed_grad(start, size, n, w_qkv, d_qkv, d_normed):
     cols = pl.ds(pl.multiple_of(n * 256, 256), 256)
-    d_normed[:, cols] = dot(d_qkv[...], w_qkv[cols, :], NT)
-
-
-def token_grad(x, inv_rms, d_normed, d_ext):
+    d_normed[start : start + size, cols] = dot(d_qkv[start : start + size, :], w_qkv[cols, :], NT)
+
+
+def token_grad(strips, x, inv_rms, d_normed, d_ext):
     def strip(s, _):
         rows = pl.ds(pl.multiple_of(s * STRIP, 16), STRIP)
         xf = x[rows, :].astype(F32)
@@ -191,7 +192,7 @@
         d_ext[pl.ds(pl.multiple_of(s * STRIP + BAND, 16), STRIP), :] = (inv * dn - xf * pull).astype(BF16)
         return 0
 
-    lax.fori_loop(0, STRIPS, strip, 0)
+    lax.fori_loop(*strips, strip, 0)
 
 
 def assemble(d_ext, d_edges, d_tokens):
@@ -267,58 +268,74 @@
         remote(edge_out, edges.at[:, 0:EDGE], halo_send, halo_recv, 2, left),
         remote(edge_out.at[:, 0:16], edges.at[:, EDGE:EDGES], halo_send, halo_recv, 3, corner),
     ]
-    halos[0].start()
-    halos[1].start()
     edge_out[0] = dot(pick, x_ext[0:LOCAL, :]).astype(BF16)
     edge_out[1] = dot(pick, cot_ext[0:LOCAL, :]).astype(BF16)
     halos[2].start()
     halos[3].start()
-    for copy in halos:
-        copy.wait_recv()
-    prologue(x_ext, cot_ext, edges, x, cot, normed, normed_t, cot_t, inv_rms)
+    halos[0].start()
+    halos[1].start()
+    halos[2].wait_recv()
+    halos[3].wait_recv()
+    early, late = (0, STRIPS - 1), (STRIPS - 1, STRIPS)
+    normalize(early, x_ext, cot_ext, edges, x, cot, normed, inv_rms)
+    turn(range(5), cot, normed, normed_t, cot_t)
     for copy in loads[2:]:
         copy.wait()
-    first = lambda p: rs_first(p, terms, got_0, got_1, send, recv)
-    second = lambda p: rs_next(p, 0, terms, got_1, sum_1, got_2, send, recv)
-    third = lambda p: rs_next(p, 1, sum_1, got_2, sum_2, got_3, send, recv)
-    last = lambda p: rs_next(p, 2, sum_2, got_3, sum_3, None, send, recv)
+    first = lambda p, half: rs_first(p, half, terms, got_0, got_1, send, recv)
+    second = lambda p, half: rs_next(p, half, 0, terms, got_1, sum_1, got_2, send, recv)
+    third = lambda p, half: rs_next(p, half, 1, sum_1, got_2, sum_2, got_3, send, recv)
+    last = lambda p, half: rs_next(p, half, 2, sum_2, got_3, sum_3, None, send, recv)
+
+    def finish_halo():
+        halos[0].wait_recv()
+        halos[1].wait_recv()
+        normalize(late, x_ext, cot_ext, edges, x, cot, normed, inv_rms)
+        turn(range(5, 7), cot, normed, normed_t, cot_t)
 
     def chunk(p, _):
-        project(p, cot, w_qkv, w_out, normed, qb, kb, vb, dab)
-        pl.when(p > 0)(lambda: first(p - 1))
-        attend(p, bias, qb, kb, vb, dab, ob, d_qkv)
-        pl.when(p > 1)(lambda: third(p - 2))
-        weight_terms(p, normed_t, cot_t, d_qkv, ob, terms)
-        rs_start(p, terms, got_0, send, recv)
-        pl.when(p > 0)(lambda: second(p - 1))
+        project(p, 0, EARLY, cot, w_qkv, w_out, normed, qb, kb, vb, dab)
+        pl.when(p > 0)(lambda: first(p - 1, 0))
+        attend(p, early, bias, qb, kb, vb, dab, ob, d_qkv)
+        pl.when(p == 0)(finish_halo)
+        pl.when(p > 0)(lambda: second(p - 1, 1))
+        project(p, EARLY, STRIP, cot, w_qkv, w_out, normed, qb, kb, vb, dab)
+        attend(p, late, bias, qb, kb, vb, dab, ob, d_qkv)
+        pl.when(p > 0)(lambda: second(p - 1, 0))
+        weight_terms(p, 1, normed_t, cot_t, d_qkv, ob, terms)
+        core_copy(p, 1, terms, got_0, send, recv).start()
+        pl.when(p > 0)(lambda: third(p - 1, 1))
+        weight_terms(p, 0, normed_t, cot_t, d_qkv, ob, terms)
+        core_copy(p, 0, terms, got_0, send, recv).start()
+        pl.when(p > 0)(lambda: third(p - 1, 0))
+        first(p, 1)
         return 0
 
     lax.fori_loop(0, CHUNKS, chunk, 0)
-
-    def tail(n, _):
-        normed_grad(n, w_qkv, d_qkv, d_normed)
-        pl.when(n == 0)(lambda: first(CHUNKS - 1))
-        pl.when(n == 1)(lambda: third(CHUNKS - 2))
-        return 0
-
-    lax.fori_loop(0, D // 256, tail, 0)
-    token_grad(x, inv_rms, d_normed, d_ext)
+    end = CHUNKS - 1
     down, right, far_corner = neighbour(1, 0), neighbour(0, 1), neighbour(1, 1)
     returns = [
         remote(d_ext.at[LOCAL : LOCAL + BAND], d_ext.at[0:BAND], halo_send, halo_recv, 4, down),
         remote(d_edge_out, d_edges.at[0:EDGE], halo_send, halo_recv, 5, right),
         remote(d_edge_out.at[EDGE - 16 : EDGE], d_edges.at[EDGE:EDGES], halo_send, halo_recv, 6, far_corner),
     ]
+    lax.fori_loop(0, D // 256, lambda n, _: (normed_grad(EARLY, STRIP, n, w_qkv, d_qkv, d_normed), 0)[1], 0)
+    first(end, 0)
+    token_grad(late, x, inv_rms, d_normed, d_ext)
     returns[0].start()
+    lax.fori_loop(0, D // 256, lambda n, _: (normed_grad(0, EARLY, n, w_qkv, d_qkv, d_normed), 0)[1], 0)
+    token_grad(early, x, inv_rms, d_normed, d_ext)
     d_edge_out[...] = dot(edge_pick(), d_ext[BAND : BAND + LOCAL, :]).astype(BF16)
     returns[1].start()
     returns[2].start()
-    second(CHUNKS - 1)
+    second(end, 1)
+    second(end, 0)
     for copy in returns:
         copy.wait_recv()
     assemble(d_ext, d_edges, d_tokens)
-    third(CHUNKS - 1)
-    lax.fori_loop(0, CHUNKS, lambda p, _: (last(p), 0)[1], 0)
+    third(end, 1)
+    third(end, 0)
+    for half in (0, 1):
+        lax.fori_loop(0, CHUNKS, lambda p, _: (last(p, half), 0)[1], 0)
     write_grads(sum_3, grad_qkv, grad_out)
     rs_finish(terms, got_0, (terms, sum_1, sum_2), (got_1, got_2, got_3), send, recv)
     for copy in halos + returns:
@@ -417,13 +434,13 @@
     pl.semaphore_wait(pltpu.get_barrier_semaphore(), 10 + len(AROUND))
 
 
-def core_copy(p, terms, got_0, send, recv):
+def core_copy(p, half, terms, got_0, send, recv):
     x, y, z, core = place()
     return pltpu.make_async_remote_copy(
-        src_ref=terms.at[p, 1 - core],
-        dst_ref=got_0.at[p],
-        send_sem=send.at[p, 0, 0],
-        recv_sem=recv.at[p, 0, 0],
+        src_ref=terms.at[p, 1 - core, half],
+        dst_ref=got_0.at[p, half],
+        send_sem=send.at[p, 0, half],
+        recv_sem=recv.at[p, 0, half],
         device_id=device(x, y, z, 1 - core),
         device_id_type=MESH,
     )
@@ -450,37 +467,32 @@
     return {"x": x, "y": y, "z": z}[ORDERS[half][stage]]
 
 
-def rs_start(p, terms, got_0, send, recv):
-    core_copy(p, terms, got_0, send, recv).start()
-
-
-def rs_first(p, terms, got_0, got_1, send, recv):
+def rs_first(p, half, terms, got_0, got_1, send, recv):
     core = place()[3]
-    core_copy(p, terms, got_0, send, recv).wait_recv()
-    for half in (0, 1):
-        for a in range(4):
-            terms[p, core, half, a] = terms[p, core, half, a] + got_0[p, half, a]
-    for half, step in STEPS:
+    core_copy(p, half, terms, got_0, send, recv).wait_recv()
+    for a in range(4):
+        terms[p, core, half, a] = terms[p, core, half, a] + got_0[p, half, a]
+    for step in (2, 1, 3):
         stage_copy(p, 0, half, step, terms, got_1, send, recv).start()
 
 
-def rs_next(p, stage, source, got, total, after, send, recv):
-    for half, step in STEPS:
+def rs_next(p, half, stage, source, got, total, after, send, recv):
+    for step in (1, 2, 3):
         stage_copy(p, stage, half, step, source, got, send, recv).wait_recv()
-    for half in (0, 1):
-        index = (half, my_index(stage, half))
-        mine = source[(p, place()[3]) + index if stage == 0 else (p,) + index].astype(F32)
-        for i in range(3):
-            mine = mine + got[p, half, i].astype(F32)
-        total[p, half] = mine.astype(total.dtype)
+    index = (half, my_index(stage, half))
+    mine = source[(p, place()[3]) + index if stage == 0 else (p,) + index].astype(F32)
+    for i in range(3):
+        mine = mine + got[p, half, i].astype(F32)
+    total[p, half] = mine.astype(total.dtype)
     if after is not None:
-        for half, step in STEPS:
+        for step in (2, 1, 3):
             stage_copy(p, stage + 1, half, step, total, after, send, recv).start()
 
 
 def rs_finish(terms, got_0, sums, gots, send, recv):
     def one(p, _):
-        core_copy(p, terms, got_0, send, recv).wait_send()
+        for half in (0, 1):
+            core_copy(p, half, terms, got_0, send, recv).wait_send()
         for stage in range(3):
             for half, step in STEPS:
                 stage_copy(p, stage, half, step, sums[stage], gots[stage], send, recv).wait_send()

time: 113 us -> 112 us (level)
  no operation moved by 1% of the time
where the time goes in v4:
time: 112 us
  Pallas kernels  108 us (96%)
  local copies, waits for them, and re-layouts  4.12 us (4%)
    pallas_call x1, Pallas kernels, window_call(): pl.pallas_call(window_kernel, out_shape=(jax.ShapeDtypeStruct((LOCAL, D),...  108 us
    unnamed x7, local copies, waits for them, and re-layouts  4.12 us

profile of v4, /device:TPU:1, one launch (start us, length us, event | category | flops | bytes accessed | tf_op | source)
XLA Modules:
  0.0 112.3 jit_solution(1070145675205708825)
XLA Ops:
  0.6 107.5 %windows.1 = (bf16[864,1024]{1,0:T(8,128)(2,1)}, f32[8,3072]{1,0:T(8,128)}, f32[8,1024]{1,0:T(8,128)}) custom-call(bf16[864,1024]{1,0:T(8,128)(2,1)} %bitcast.3, bf16[864,1024]{1,0:T(8,128)(2,1)} %bitcast.4, bf16[1024,3072]{1,0:T(8,128)(2,1)} %w_qkv_hbm.1, bf16[1024,1024]{1,0:T(8,128)(2,1)} %w_out_hbm.1, s32[288]{0:T(512)} %row_valid.1), custom_call_target="tpu_custom_call" | custom-call | tf_op jit(solution)/shard_map/windows/pallas_call | solution.py:351
  108.1 0.0 copy-start
  108.2 0.0 copy-start.1
  108.2 2.9 %copy.11 = bf16[36,24,1024]{2,1,0:T(8,128)(2,1)} copy(bf16[36,24,1024]{2,1,0:T(8,128)(2,1)} %bitcast.5) | data formatting | bytes 3538944
  111.0 0.0 copy-done
  111.0 0.6 copy.12
  111.7 0.0 copy-done.1
  111.7 0.6 copy.13
Async XLA Ops:
  108.1 2.9 %copy-start = (f32[8,3072]{1,0:T(8,128)S(1)}, f32[8,3072]{1,0:T(8,128)}, u32[]{:S(2)}) copy-start(f32[8,3072]{1,0:T(8,128)} %get-tuple-element.13) | copy-start | bytes 294916
  108.2 3.5 %copy-start.1 = (f32[8,1024]{1,0:T(8,128)S(1)}, f32[8,1024]{1,0:T(8,128)}, u32[]{:S(2)}) copy-start(f32[8,1024]{1,0:T(8,128)} %get-tuple-element.14) | copy-start | bytes 98308

commit v5 on v4

--- a/solution.py
+++ b/solution.py
@@ -72,22 +72,29 @@
     return jnp.where(token == at // HALF * COLS + at % HALF, 1.0, 0.0).astype(BF16)
 
 
-def edge_spread(s, near, far):
-    token = lax.broadcasted_iota(jnp.int32, (STRIP, EDGES), 0)
-    at = lax.broadcasted_iota(jnp.int32, (STRIP, EDGES), 1)
+def corner_pick():
+    at = lax.broadcasted_iota(jnp.int32, (16, STRIP), 0) - HALF
+    token = lax.broadcasted_iota(jnp.int32, (16, STRIP), 1)
+    source = (HALF + (at + HALF) // HALF - 1) * COLS + (at + HALF) % HALF
+    return jnp.where((at >= 0) & (at < HALF * HALF) & (token == source), 1.0, 0.0).astype(BF16)
+
+
+def edge_spread(s, near, far, width=EDGES):
+    token = lax.broadcasted_iota(jnp.int32, (STRIP, width), 0)
+    at = lax.broadcasted_iota(jnp.int32, (STRIP, width), 1)
     row, col = s * WIN + token // COLS, token % COLS
     source = jnp.where(near(row), far[0] + HALF * row + col, far[1] + HALF * row + col)
     return jnp.where((col < HALF) & (at == source), 1.0, 0.0).astype(BF16)
 
 
-def normalize(strips, x_ext, cot_ext, edges, x, cot, normed, inv_rms):
+def normalize(strips, width, x_ext, cot_ext, edges, x, cot, normed, inv_rms):
     is_edge = lax.broadcasted_iota(jnp.int32, (STRIP, 1), 0) % COLS < HALF
 
     def norm_strip(s, _):
         rows = pl.ds(pl.multiple_of(s * STRIP, 16), STRIP)
-        spread = edge_spread(s, lambda row: row < ROWS - HALF, (HALF * HALF, EDGE - HALF * (ROWS - HALF)))
-        cot[rows, :] = jnp.where(is_edge, dot(spread, edges[1]), shift_rows(cot_ext, s)).astype(BF16)
-        xf = jnp.where(is_edge, dot(spread, edges[0]), shift_rows(x_ext, s))
+        spread = edge_spread(s, lambda row: row < ROWS - HALF, (HALF * HALF, EDGE - HALF * (ROWS - HALF)), width)
+        cot[rows, :] = jnp.where(is_edge, dot(spread, edges[1, 0:width, :]), shift_rows(cot_ext, s)).astype(BF16)
+        xf = jnp.where(is_edge, dot(spread, edges[0, 0:width, :]), shift_rows(x_ext, s))
         x[rows, :] = xf.astype(BF16)
         inv = lax.rsqrt(jnp.mean(xf * xf, axis=-1, keepdims=True) + EPSILON)
         inv_rms[rows, :] = inv
@@ -115,7 +122,7 @@
     dab[rows, :] = dot(cot[rows, :], w_out[pl.ds(base, GROUP), :], NT).astype(BF16)
 
 
-def attend(p, strips, bias, qb, kb, vb, dab, ob, d_qkv):
+def attend(p, strips, unroll, bias, qb, kb, vb, dab, ob, d_qkv):
     row_head = lax.broadcasted_iota(jnp.int32, (GROUP, GROUP), 0) // HEAD_DIM
     col_head = lax.broadcasted_iota(jnp.int32, (GROUP, GROUP), 1) // HEAD_DIM
     ones = jnp.where(row_head == col_head, 1.0, 0.0).astype(BF16)
@@ -152,29 +159,25 @@
         d_qkv[rows, pl.ds(base + D, GROUP)] = d_k.astype(BF16)
         return 0
 
-    lax.fori_loop(*strips, strip, 0, unroll=strips[1] - strips[0])
+    lax.fori_loop(*strips, strip, 0, unroll=unroll)
 
 
 def weight_terms(p, half, normed_t, cot_t, d_qkv, ob, terms):
-    def plane(z, _):
-        rows = pl.ds(pl.multiple_of(z * 256, 256), 256)
-        base = pl.multiple_of(p * GROUP, GROUP)
-        n = normed_t[rows, :]
+    base = pl.multiple_of(p * GROUP, GROUP)
+    for top in range(0, D, 512):
+        n = normed_t[top : top + 512, :]
         if half == 0:
             upper = dot(n, d_qkv[:, pl.ds(base, GROUP)])
             lower = dot(n, d_qkv[:, pl.ds(base + D, GROUP)])
         else:
             upper = dot(n, d_qkv[:, pl.ds(base + 2 * D, GROUP)])
-            lower = dot(cot_t[rows, :], ob[...])
-        for unit in range(32):
-            y_lo, core, x, y_hi = unit // 16, unit // 8 % 2, unit // 2 % 4, unit % 2
+            lower = dot(cot_t[top : top + 512, :], ob[...])
+        for at in range(0, 512, 8):
+            unit = (top + at) // 8
+            z, y_lo, core, x, y_hi = unit // 32, unit // 16 % 2, unit // 8 % 2, unit // 2 % 4, unit % 2
             y = y_hi * 2 + y_lo
-            part = slice(unit * 8, unit * 8 + 8)
-            both = jnp.concatenate([upper[part], lower[part]], axis=0).astype(BF16)
+            both = jnp.concatenate([upper[at : at + 8], lower[at : at + 8]], axis=0).astype(BF16)
             terms[(p, core, half) + ((x, y, z) if half == 0 else (z, y, x))] = both
-        return 0
-
-    lax.fori_loop(0, 4, plane, 0)
 
 
 def normed_grad(start, size, n, w_qkv, d_qkv, d_normed):
@@ -243,7 +246,7 @@
 
 def window_kernel(
     tokens, cotangent, w_qkv_hbm, w_out_hbm, row_valid, d_tokens, grad_qkv, grad_out,
-    x_ext, cot_ext, w_qkv, w_out, edge_out, edges, d_ext, d_edge_out, d_edges,
+    x_ext, cot_ext, w_qkv, w_out, edge_out, edges, d_ext, d_edge_out, d_corner_out, d_edges,
     bias, x, cot, normed, normed_t, cot_t, inv_rms, qb, kb, vb, dab, ob, d_qkv, d_normed, terms,
     got_0, got_1, sum_1, got_2, sum_2, got_3, sum_3, send, recv, halo_send, halo_recv, load,
 ):
@@ -275,9 +278,8 @@
     halos[0].start()
     halos[1].start()
     halos[2].wait_recv()
-    halos[3].wait_recv()
     early, late = (0, STRIPS - 1), (STRIPS - 1, STRIPS)
-    normalize(early, x_ext, cot_ext, edges, x, cot, normed, inv_rms)
+    normalize(early, EDGE, x_ext, cot_ext, edges, x, cot, normed, inv_rms)
     turn(range(5), cot, normed, normed_t, cot_t)
     for copy in loads[2:]:
         copy.wait()
@@ -287,26 +289,37 @@
     last = lambda p, half: rs_next(p, half, 2, sum_2, got_3, sum_3, None, send, recv)
 
     def finish_halo():
-        halos[0].wait_recv()
-        halos[1].wait_recv()
-        normalize(late, x_ext, cot_ext, edges, x, cot, normed, inv_rms)
+        for i in (0, 1, 3):
+            halos[i].wait_recv()
+        normalize(late, EDGES, x_ext, cot_ext, edges, x, cot, normed, inv_rms)
         turn(range(5, 7), cot, normed, normed_t, cot_t)
 
+    def both_thirds(p):
+        third(p, 1)
+        third(p, 0)
+
+    def parts(p):
+        project(p, 0, EARLY, cot, w_qkv, w_out, normed, qb, kb, vb, dab)
+        attend(p, early, 5, bias, qb, kb, vb, dab, ob, d_qkv)
+        finish_halo()
+        project(p, EARLY, STRIP, cot, w_qkv, w_out, normed, qb, kb, vb, dab)
+        attend(p, late, 1, bias, qb, kb, vb, dab, ob, d_qkv)
+
+    def whole(p):
+        project(p, 0, LOCAL, cot, w_qkv, w_out, normed, qb, kb, vb, dab)
+        first(p - 1, 0)
+        attend(p, (0, STRIPS), 3, bias, qb, kb, vb, dab, ob, d_qkv)
+        second(p - 1, 1)
+        pl.when(p > 1)(lambda: both_thirds(p - 2))
+
     def chunk(p, _):
-        project(p, 0, EARLY, cot, w_qkv, w_out, normed, qb, kb, vb, dab)
-        pl.when(p > 0)(lambda: first(p - 1, 0))
-        attend(p, early, bias, qb, kb, vb, dab, ob, d_qkv)
-        pl.when(p == 0)(finish_halo)
-        pl.when(p > 0)(lambda: second(p - 1, 1))
-        project(p, EARLY, STRIP, cot, w_qkv, w_out, normed, qb, kb, vb, dab)
-        attend(p, late, bias, qb, kb, vb, dab, ob, d_qkv)
-        pl.when(p > 0)(lambda: second(p - 1, 0))
+        pl.when(p == 0)(lambda: parts(p))
+        pl.when(p > 0)(lambda: whole(p))
         weight_terms(p, 1, normed_t, cot_t, d_qkv, ob, terms)
         core_copy(p, 1, terms, got_0, send, recv).start()
-        pl.when(p > 0)(lambda: third(p - 1, 1))
+        pl.when(p > 0)(lambda: second(p - 1, 0))
         weight_terms(p, 0, normed_t, cot_t, d_qkv, ob, terms)
         core_copy(p, 0, terms, got_0, send, recv).start()
-        pl.when(p > 0)(lambda: third(p - 1, 0))
         first(p, 1)
         return 0
 
@@ -316,17 +329,19 @@
     returns = [
         remote(d_ext.at[LOCAL : LOCAL + BAND], d_ext.at[0:BAND], halo_send, halo_recv, 4, down),
         remote(d_edge_out, d_edges.at[0:EDGE], halo_send, halo_recv, 5, right),
-        remote(d_edge_out.at[EDGE - 16 : EDGE], d_edges.at[EDGE:EDGES], halo_send, halo_recv, 6, far_corner),
+        remote(d_corner_out, d_edges.at[EDGE:EDGES], halo_send, halo_recv, 6, far_corner),
     ]
     lax.fori_loop(0, D // 256, lambda n, _: (normed_grad(EARLY, STRIP, n, w_qkv, d_qkv, d_normed), 0)[1], 0)
     first(end, 0)
+    both_thirds(end - 1)
     token_grad(late, x, inv_rms, d_normed, d_ext)
+    d_corner_out[...] = dot(corner_pick(), d_ext[BAND + EARLY : BAND + LOCAL, :]).astype(BF16)
+    returns[2].start()
     returns[0].start()
     lax.fori_loop(0, D // 256, lambda n, _: (normed_grad(0, EARLY, n, w_qkv, d_qkv, d_normed), 0)[1], 0)
     token_grad(early, x, inv_rms, d_normed, d_ext)
     d_edge_out[...] = dot(edge_pick(), d_ext[BAND : BAND + LOCAL, :]).astype(BF16)
     returns[1].start()
-    returns[2].start()
     second(end, 1)
     second(end, 0)
     for copy in returns:
@@ -366,6 +381,7 @@
             pltpu.VMEM((2, EDGES, D), BF16),
             pltpu.VMEM((BAND + LOCAL, D), BF16),
             pltpu.VMEM((EDGE, D), BF16),
+            pltpu.VMEM((16, D), BF16),
             pltpu.VMEM((EDGES, D), BF16),
             pltpu.VMEM((STRIPS, STRIP, STRIP), F32),
             pltpu.VMEM((LOCAL, D), BF16),

time: 112 us -> 103 us (0.920)
  Pallas kernels: 108 us -> 97.8 us
    pallas_call x1, Pallas kernels: 108 us -> 97.8 us  [window_call(): pl.pallas_call(window_kernel, out_shape=(jax.ShapeDtypeStruct((LOCAL, D),...]
where the time goes in v5:
time: 103 us
  Pallas kernels  97.8 us (95%)
  local copies, waits for them, and re-layouts  4.12 us (4%)
    pallas_call x1, Pallas kernels, window_call(): pl.pallas_call(window_kernel, out_shape=(jax.ShapeDtypeStruct((LOCAL, D),...  97.8 us
    unnamed x7, local copies, waits for them, and re-layouts  4.12 us

profile of v5, /device:TPU:1, one launch (start us, length us, event | category | flops | bytes accessed | tf_op | source)
XLA Modules:
  0.0 102.5 jit_solution(9715125280503753054)
XLA Ops:
  0.6 97.8 %windows.1 = (bf16[864,1024]{1,0:T(8,128)(2,1)}, f32[8,3072]{1,0:T(8,128)}, f32[8,1024]{1,0:T(8,128)}) custom-call(bf16[864,1024]{1,0:T(8,128)(2,1)} %bitcast.3, bf16[864,1024]{1,0:T(8,128)(2,1)} %bitcast.4, bf16[1024,3072]{1,0:T(8,128)(2,1)} %w_qkv_hbm.1, bf16[1024,1024]{1,0:T(8,128)(2,1)} %w_out_hbm.1, s32[288]{0:T(512)} %row_valid.1), custom_call_target="tpu_custom_call" | custom-call | tf_op jit(solution)/shard_map/windows/pallas_call | solution.py:366
  98.4 0.0 copy-start
  98.4 0.0 copy-start.1
  98.4 2.9 %copy.11 = bf16[36,24,1024]{2,1,0:T(8,128)(2,1)} copy(bf16[36,24,1024]{2,1,0:T(8,128)(2,1)} %bitcast.5) | data formatting | bytes 3538944
  101.3 0.0 copy-done
  101.3 0.6 copy.12
  101.9 0.0 copy-done.1
  101.9 0.6 copy.13
Async XLA Ops:
  98.4 2.9 %copy-start = (f32[8,3072]{1,0:T(8,128)S(1)}, f32[8,3072]{1,0:T(8,128)}, u32[]{:S(2)}) copy-start(f32[8,3072]{1,0:T(8,128)} %get-tuple-element.13) | copy-start | bytes 294916
  98.4 3.5 %copy-start.1 = (f32[8,1024]{1,0:T(8,128)S(1)}, f32[8,1024]{1,0:T(8,128)}, u32[]{:S(2)}) copy-start(f32[8,1024]{1,0:T(8,128)} %get-tuple-element.14) | copy-start | bytes 98308

commit v6 on v5

--- a/solution.py
+++ b/solution.py
@@ -245,10 +245,10 @@
 
 
 def window_kernel(
-    tokens, cotangent, w_qkv_hbm, w_out_hbm, row_valid, d_tokens, grad_qkv, grad_out,
+    tokens, cotangent, w_qkv_hbm, w_out_hbm, row_valid, d_ext_hbm, d_edges_hbm, sum_3,
     x_ext, cot_ext, w_qkv, w_out, edge_out, edges, d_ext, d_edge_out, d_corner_out, d_edges,
     bias, x, cot, normed, normed_t, cot_t, inv_rms, qb, kb, vb, dab, ob, d_qkv, d_normed, terms,
-    got_0, got_1, sum_1, got_2, sum_2, got_3, sum_3, send, recv, halo_send, halo_recv, load,
+    got_0, got_1, sum_1, got_2, sum_2, got_3, send, recv, halo_send, halo_recv, load,
 ):
     greet()
     loads = [
@@ -340,21 +340,56 @@
     returns[0].start()
     lax.fori_loop(0, D // 256, lambda n, _: (normed_grad(0, EARLY, n, w_qkv, d_qkv, d_normed), 0)[1], 0)
     token_grad(early, x, inv_rms, d_normed, d_ext)
+    second(end, 1)
     d_edge_out[...] = dot(edge_pick(), d_ext[BAND : BAND + LOCAL, :]).astype(BF16)
     returns[1].start()
-    second(end, 1)
+    stores = [
+        pltpu.make_async_copy(d_ext.at[BAND : BAND + LOCAL], d_ext_hbm.at[BAND : BAND + LOCAL], load.at[0]),
+        pltpu.make_async_copy(d_ext.at[0:BAND], d_ext_hbm.at[0:BAND], load.at[1]),
+        pltpu.make_async_copy(d_edges, d_edges_hbm, load.at[2]),
+    ]
+    stores[0].start()
     second(end, 0)
+
+    def settle(p, _):
+        last(p, 1)
+        last(p, 0)
+        rs_finish(p, terms, got_0, (terms, sum_1, sum_2), (got_1, got_2, got_3), send, recv)
+        return 0
+
+    lax.fori_loop(0, end, settle, 0)
+    third(end, 1)
     for copy in returns:
         copy.wait_recv()
-    assemble(d_ext, d_edges, d_tokens)
-    third(end, 1)
+    stores[1].start()
+    stores[2].start()
     third(end, 0)
-    for half in (0, 1):
-        lax.fori_loop(0, CHUNKS, lambda p, _: (last(p, half), 0)[1], 0)
-    write_grads(sum_3, grad_qkv, grad_out)
-    rs_finish(terms, got_0, (terms, sum_1, sum_2), (got_1, got_2, got_3), send, recv)
     for copy in halos + returns:
         copy.wait_send()
+    settle(end, 0)
+    for copy in stores:
+        copy.wait()
+
+
+def place_kernel(d_ext, d_edges, sum_3, d_tokens, grad_qkv, grad_out):
+    assemble(d_ext, d_edges, d_tokens)
+    write_grads(sum_3, grad_qkv, grad_out)
+
+
+def place_call(d_ext, d_edges, sum_3):
+    vmem = pl.BlockSpec(memory_space=pltpu.VMEM)
+    return pl.pallas_call(
+        place_kernel,
+        out_shape=(
+            jax.ShapeDtypeStruct((LOCAL, D), BF16),
+            jax.ShapeDtypeStruct((8, 3 * D), F32),
+            jax.ShapeDtypeStruct((8, D), F32),
+        ),
+        in_specs=[vmem] * 3,
+        out_specs=(vmem, vmem, vmem),
+        compiler_params=pltpu.CompilerParams(vmem_limit_bytes=62 * 1024 * 1024),
+        name="assembly",
+    )(d_ext, d_edges, sum_3)
 
 
 TERMS = (CHUNKS, 2, 2, 4, 4, 4, 16, GROUP)
@@ -366,12 +401,12 @@
     return pl.pallas_call(
         window_kernel,
         out_shape=(
-            jax.ShapeDtypeStruct((LOCAL, D), BF16),
-            jax.ShapeDtypeStruct((8, 3 * D), F32),
-            jax.ShapeDtypeStruct((8, D), F32),
+            jax.ShapeDtypeStruct((BAND + LOCAL, D), BF16),
+            jax.ShapeDtypeStruct((EDGES, D), BF16),
+            jax.ShapeDtypeStruct((CHUNKS, 2, 16, GROUP), F32),
         ),
         in_specs=[anywhere] * 4 + [pl.BlockSpec(memory_space=pltpu.SMEM)],
-        out_specs=(vmem, vmem, vmem),
+        out_specs=(anywhere, anywhere, vmem),
         scratch_shapes=[
             pltpu.VMEM((LOCAL + BAND, D), BF16),
             pltpu.VMEM((LOCAL + BAND, D), BF16),
@@ -505,16 +540,12 @@
             stage_copy(p, stage + 1, half, step, total, after, send, recv).start()
 
 
-def rs_finish(terms, got_0, sums, gots, send, recv):
-    def one(p, _):
-        for half in (0, 1):
-            core_copy(p, half, terms, got_0, send, recv).wait_send()
-        for stage in range(3):
-            for half, step in STEPS:
-                stage_copy(p, stage, half, step, sums[stage], gots[stage], send, recv).wait_send()
-        return 0
-
-    lax.fori_loop(0, CHUNKS, one, 0)
+def rs_finish(p, terms, got_0, sums, gots, send, recv):
+    for half in (0, 1):
+        core_copy(p, half, terms, got_0, send, recv).wait_send()
+    for stage in range(3):
+        for half, step in STEPS:
+            stage_copy(p, stage, half, step, sums[stage], gots[stage], send, recv).wait_send()
 
 
 def write_grads(sum_3, grad_qkv, grad_out):
@@ -536,7 +567,6 @@
         pltpu.VMEM((CHUNKS, 2, 3, 4) + unit, BF16),
         pltpu.VMEM((CHUNKS, 2, 4) + unit, BF16),
         pltpu.VMEM((CHUNKS, 2, 3) + unit, BF16),
-        pltpu.VMEM((CHUNKS, 2) + unit, F32),
         pltpu.SemaphoreType.DMA((CHUNKS, 4, 6)),
         pltpu.SemaphoreType.DMA((CHUNKS, 4, 6)),
     ]
@@ -544,7 +574,9 @@
 
 def on_device(tokens, cotangent, w_qkv, w_out, row_valid):
     flat = (LOCAL, D)
-    d_tokens, grad_qkv, grad_out = window_call(tokens.reshape(flat), cotangent.reshape(flat), w_qkv, w_out, row_valid)
+    d_tokens, grad_qkv, grad_out = place_call(
+        *window_call(tokens.reshape(flat), cotangent.reshape(flat), w_qkv, w_out, row_valid)
+    )
     return (d_tokens.reshape(tokens.shape), grad_qkv, grad_out)
 
 

time: 103 us -> 102 us (level)
  local copies, waits for them, and re-layouts: 4.12 us -> 0 us
  Pallas kernels: 97.8 us -> 101 us
    unnamed x7 -> x0, local copies, waits for them, and re-layouts: 4.12 us -> none
    pallas_call x1 -> x2, Pallas kernels: 97.8 us -> 101 us  [the longest x1 97 us: window_call(): pl.pallas_call(window_kernel, out_shape=(jax.ShapeDtypeStruct((BAND + LOC...]
where the time goes in v6:
time: 102 us
  Pallas kernels  101 us (99%)
    pallas_call x1, Pallas kernels, window_call(): pl.pallas_call(window_kernel, out_shape=(jax.ShapeDtypeStruct((BAND + LOC...  97 us
    pallas_call x1, Pallas kernels, place_call(): pl.pallas_call(place_kernel, out_shape=(jax.ShapeDtypeStruct((LOCAL, D),...  4.25 us

profile of v6, /device:TPU:1, one launch (start us, length us, event | category | flops | bytes accessed | tf_op | source)
XLA Modules:
  0.0 101.9 jit_solution(3423605050949464626)
XLA Ops:
  0.6 97.0 %windows.1 = (bf16[944,1024]{1,0:T(8,128)(2,1)}, bf16[128,1024]{1,0:T(8,128)(2,1)}, f32[4,2,16,256]{3,2,1,0:T(8,128)}) custom-call(bf16[864,1024]{1,0:T(8,128)(2,1)} %bitcast.3, bf16[864,1024]{1,0:T(8,128)(2,1)} %bitcast.4, bf16[1024,3072]{1,0:T(8,128)(2,1)} %w_qkv_hbm.1, bf16[1024,1024]{1,0:T(8,128)(2,1)} %w_out_hbm.1, s32[288]{0:T(512)} %row_valid.1), custom_call_target="tpu_custom_call" | custom-call | tf_op jit(solution)/shard_map/windows/pallas_call | solution.py:401
  97.7 4.3 %assembly.1 = (bf16[864,1024]{1,0:T(8,128)(2,1)}, f32[8,3072]{1,0:T(8,128)}, f32[8,1024]{1,0:T(8,128)}) custom-call(bf16[944,1024]{1,0:T(8,128)(2,1)} %get-tuple-element.9.d_ext, bf16[128,1024]{1,0:T(8,128)(2,1)} %get-tuple-element.10.d_edges, f32[4,2,16,256]{3,2,1,0:T(8,128)} %get-tuple-element.11.sum_3), custom_call_target="tpu_custom_call" | custom-call | tf_op jit(solution)/shard_map/assembly/pallas_call | solution.py:381

commit v7 on v6

--- a/solution.py
+++ b/solution.py
@@ -24,6 +24,7 @@
 EDGE = 112
 EDGES = 128
 BAND = 80
+PLACED = 2
 EARLY = STRIP * (STRIPS - 1)
 
 SHARP = 10.0
@@ -198,17 +199,14 @@
     lax.fori_loop(*strips, strip, 0)
 
 
-def assemble(d_ext, d_edges, d_tokens):
+def assemble(d_ext, d_next, d_edges, d_tokens):
     is_edge = lax.broadcasted_iota(jnp.int32, (STRIP, 1), 0) % COLS < HALF
-
-    def strip(s, _):
-        start = pl.multiple_of(s * STRIP, 16)
-        own = d_ext[pl.ds(start, STRIP + 16), :].astype(F32)[8 : 8 + STRIP]
+    held = jnp.concatenate([d_ext[...].astype(F32), d_next[...].astype(F32)], axis=0)
+    for i in range(PLACED):
+        s = pl.program_id(0) * PLACED + i
         spread = edge_spread(s, lambda row: row >= HALF, (-HALF * HALF, EDGE + HALF))
-        d_tokens[pl.ds(start, STRIP), :] = jnp.where(is_edge, dot(spread, d_edges[...]), own).astype(BF16)
-        return 0
-
-    lax.fori_loop(0, STRIPS, strip, 0)
+        own = held[i * STRIP + 8 : (i + 1) * STRIP + 8]
+        d_tokens[i * STRIP : (i + 1) * STRIP, :] = jnp.where(is_edge, dot(spread, d_edges[...]), own).astype(BF16)
 
 
 def pair_bias(row_valid, bias):
@@ -263,6 +261,8 @@
     pick = edge_pick()
     for copy in loads[:2]:
         copy.wait()
+    edge_out[0] = dot(pick, x_ext[0:LOCAL, :]).astype(BF16)
+    edge_out[1] = dot(pick, cot_ext[0:LOCAL, :]).astype(BF16)
     met()
     up, left, corner = neighbour(-1, 0), neighbour(0, -1), neighbour(-1, -1)
     halos = [
@@ -271,8 +271,6 @@
         remote(edge_out, edges.at[:, 0:EDGE], halo_send, halo_recv, 2, left),
         remote(edge_out.at[:, 0:16], edges.at[:, EDGE:EDGES], halo_send, halo_recv, 3, corner),
     ]
-    edge_out[0] = dot(pick, x_ext[0:LOCAL, :]).astype(BF16)
-    edge_out[1] = dot(pick, cot_ext[0:LOCAL, :]).astype(BF16)
     halos[2].start()
     halos[3].start()
     halos[0].start()
@@ -308,7 +306,7 @@
     def whole(p):
         project(p, 0, LOCAL, cot, w_qkv, w_out, normed, qb, kb, vb, dab)
         first(p - 1, 0)
-        attend(p, (0, STRIPS), 3, bias, qb, kb, vb, dab, ob, d_qkv)
+        attend(p, (0, STRIPS), 6, bias, qb, kb, vb, dab, ob, d_qkv)
         second(p - 1, 1)
         pl.when(p > 1)(lambda: both_thirds(p - 2))
 
@@ -317,9 +315,9 @@
         pl.when(p > 0)(lambda: whole(p))
         weight_terms(p, 1, normed_t, cot_t, d_qkv, ob, terms)
         core_copy(p, 1, terms, got_0, send, recv).start()
-        pl.when(p > 0)(lambda: second(p - 1, 0))
         weight_terms(p, 0, normed_t, cot_t, d_qkv, ob, terms)
         core_copy(p, 0, terms, got_0, send, recv).start()
+        pl.when(p > 0)(lambda: second(p - 1, 0))
         first(p, 1)
         return 0
 
@@ -371,25 +369,35 @@
         copy.wait()
 
 
-def place_kernel(d_ext, d_edges, sum_3, d_tokens, grad_qkv, grad_out):
-    assemble(d_ext, d_edges, d_tokens)
-    write_grads(sum_3, grad_qkv, grad_out)
+def place_kernel(d_ext, d_next, d_edges, sum_3, d_tokens, grad_qkv, grad_out):
+    assemble(d_ext, d_next, d_edges, d_tokens)
+    pl.when(pl.program_id(0) == 0)(lambda: write_grads(sum_3, grad_qkv, grad_out))
 
 
 def place_call(d_ext, d_edges, sum_3):
-    vmem = pl.BlockSpec(memory_space=pltpu.VMEM)
+    rows = PLACED * STRIP
     return pl.pallas_call(
         place_kernel,
+        grid=(STRIPS // PLACED,),
         out_shape=(
             jax.ShapeDtypeStruct((LOCAL, D), BF16),
             jax.ShapeDtypeStruct((8, 3 * D), F32),
             jax.ShapeDtypeStruct((8, D), F32),
         ),
-        in_specs=[vmem] * 3,
-        out_specs=(vmem, vmem, vmem),
+        in_specs=[
+            pl.BlockSpec((rows, D), lambda k: (k, 0)),
+            pl.BlockSpec((16, D), lambda k: ((k + 1) * (rows // 16), 0)),
+            pl.BlockSpec((EDGES, D), lambda k: (0, 0)),
+            pl.BlockSpec((CHUNKS, 2, 16, GROUP), lambda k: (0, 0, 0, 0)),
+        ],
+        out_specs=(
+            pl.BlockSpec((rows, D), lambda k: (k, 0)),
+            pl.BlockSpec((8, 3 * D), lambda k: (0, 0)),
+            pl.BlockSpec((8, D), lambda k: (0, 0)),
+        ),
         compiler_params=pltpu.CompilerParams(vmem_limit_bytes=62 * 1024 * 1024),
         name="assembly",
-    )(d_ext, d_edges, sum_3)
+    )(d_ext, d_ext, d_edges, sum_3)
 
 
 TERMS = (CHUNKS, 2, 2, 4, 4, 4, 16, GROUP)

time: 102 us -> 101 us (level)
  Pallas kernels: 101 us -> 99.7 us
    pallas_call x1, Pallas kernels: 97 us -> 95.7 us  [window_call(): pl.pallas_call(window_kernel, out_shape=(jax.ShapeDtypeStruct((BAND + LOC...]
where the time goes in v7:
time: 101 us; the launch traced here: 100 us
  Pallas kernels  99.7 us (99%)
    pallas_call x1, Pallas kernels, window_call(): pl.pallas_call(window_kernel, out_shape=(jax.ShapeDtypeStruct((BAND + LOC...  95.7 us
    pallas_call x1, Pallas kernels, place_call(): pl.pallas_call(place_kernel, grid=(STRIPS // PLACED,), out_shape=(jax.Sha...  4.06 us

profile of v7, /device:TPU:1, one launch (start us, length us, event | category | flops | bytes accessed | tf_op | source)
XLA Modules:
  0.0 100.4 jit_solution(2809448226010716613)
XLA Ops:
  0.6 95.7 %windows.1 = (bf16[944,1024]{1,0:T(8,128)(2,1)}, bf16[128,1024]{1,0:T(8,128)(2,1)}, f32[4,2,16,256]{3,2,1,0:T(8,128)}) custom-call(bf16[864,1024]{1,0:T(8,128)(2,1)} %bitcast.3, bf16[864,1024]{1,0:T(8,128)(2,1)} %bitcast.4, bf16[1024,3072]{1,0:T(8,128)(2,1)} %w_qkv_hbm.1, bf16[1024,1024]{1,0:T(8,128)(2,1)} %w_out_hbm.1, s32[288]{0:T(512)} %row_valid.1), custom_call_target="tpu_custom_call" | custom-call | tf_op jit(solution)/shard_map/windows/pallas_call | solution.py:409
  96.3 4.1 %assembly.1 = (bf16[864,1024]{1,0:T(8,128)(2,1)}, f32[8,3072]{1,0:T(8,128)}, f32[8,1024]{1,0:T(8,128)}) custom-call(bf16[944,1024]{1,0:T(8,128)(2,1)} %get-tuple-element.9.d_ext.d_next, bf16[944,1024]{1,0:T(8,128)(2,1)} %get-tuple-element.9.d_ext.d_next, bf16[128,1024]{1,0:T(8,128)(2,1)} %get-tuple-element.10.d_edges, f32[4,2,16,256]{3,2,1,0:T(8,128)} %get-tuple-element.11.sum_3), custom_call_target="tpu_custom_call" | custom-call | tf_op jit(solution)/shard_map/assembly/pallas_call | solution.py:379

commit v8 on v7

--- a/solution.py
+++ b/solution.py
@@ -331,12 +331,12 @@
     ]
     lax.fori_loop(0, D // 256, lambda n, _: (normed_grad(EARLY, STRIP, n, w_qkv, d_qkv, d_normed), 0)[1], 0)
     first(end, 0)
-    both_thirds(end - 1)
     token_grad(late, x, inv_rms, d_normed, d_ext)
     d_corner_out[...] = dot(corner_pick(), d_ext[BAND + EARLY : BAND + LOCAL, :]).astype(BF16)
     returns[2].start()
     returns[0].start()
     lax.fori_loop(0, D // 256, lambda n, _: (normed_grad(0, EARLY, n, w_qkv, d_qkv, d_normed), 0)[1], 0)
+    both_thirds(end - 1)
     token_grad(early, x, inv_rms, d_normed, d_ext)
     second(end, 1)
     d_edge_out[...] = dot(edge_pick(), d_ext[BAND : BAND + LOCAL, :]).astype(BF16)

time: 101 us -> 99.9 us (0.989)
  no operation moved by 1% of the time
where the time goes in v8:
time: 99.9 us; the launch traced here: 99.7 us
  Pallas kernels  99 us (99%)
    pallas_call x1, Pallas kernels, window_call(): pl.pallas_call(window_kernel, out_shape=(jax.ShapeDtypeStruct((BAND + LOC...  95 us
    pallas_call x1, Pallas kernels, place_call(): pl.pallas_call(place_kernel, grid=(STRIPS // PLACED,), out_shape=(jax.Sha...  4.05 us

profile of v8, /device:TPU:1, one launch (start us, length us, event | category | flops | bytes accessed | tf_op | source)
XLA Modules:
  0.0 99.7 jit_solution(12777380559400459237)
XLA Ops:
  0.6 95.0 %windows.1 = (bf16[944,1024]{1,0:T(8,128)(2,1)}, bf16[128,1024]{1,0:T(8,128)(2,1)}, f32[4,2,16,256]{3,2,1,0:T(8,128)}) custom-call(bf16[864,1024]{1,0:T(8,128)(2,1)} %bitcast.3, bf16[864,1024]{1,0:T(8,128)(2,1)} %bitcast.4, bf16[1024,3072]{1,0:T(8,128)(2,1)} %w_qkv_hbm.1, bf16[1024,1024]{1,0:T(8,128)(2,1)} %w_out_hbm.1, s32[288]{0:T(512)} %row_valid.1), custom_call_target="tpu_custom_call" | custom-call | tf_op jit(solution)/shard_map/windows/pallas_call | solution.py:409
  95.6 4.1 %assembly.1 = (bf16[864,1024]{1,0:T(8,128)(2,1)}, f32[8,3072]{1,0:T(8,128)}, f32[8,1024]{1,0:T(8,128)}) custom-call(bf16[944,1024]{1,0:T(8,128)(2,1)} %get-tuple-element.9.d_ext.d_next, bf16[944,1024]{1,0:T(8,128)(2,1)} %get-tuple-element.9.d_ext.d_next, bf16[128,1024]{1,0:T(8,128)(2,1)} %get-tuple-element.10.d_edges, f32[4,2,16,256]{3,2,1,0:T(8,128)} %get-tuple-element.11.sum_3), custom_call_target="tpu_custom_call" | custom-call | tf_op jit(solution)/shard_map/assembly/pallas_call | solution.py:379

commit v9 on v8

--- a/solution.py
+++ b/solution.py
@@ -337,8 +337,8 @@
     returns[0].start()
     lax.fori_loop(0, D // 256, lambda n, _: (normed_grad(0, EARLY, n, w_qkv, d_qkv, d_normed), 0)[1], 0)
     both_thirds(end - 1)
+    second(end, 1)
     token_grad(early, x, inv_rms, d_normed, d_ext)
-    second(end, 1)
     d_edge_out[...] = dot(edge_pick(), d_ext[BAND : BAND + LOCAL, :]).astype(BF16)
     returns[1].start()
     stores = [

time: 99.9 us -> 98.7 us (0.988)
  Pallas kernels: 99 us -> 97.9 us
    pallas_call x1, Pallas kernels: 95 us -> 93.8 us  [window_call(): pl.pallas_call(window_kernel, out_shape=(jax.ShapeDtypeStruct((BAND + LOC...]
where the time goes in v9:
time: 98.7 us; the launch traced here: 98.5 us
  Pallas kernels  97.9 us (99%)
    pallas_call x1, Pallas kernels, window_call(): pl.pallas_call(window_kernel, out_shape=(jax.ShapeDtypeStruct((BAND + LOC...  93.8 us
    pallas_call x1, Pallas kernels, place_call(): pl.pallas_call(place_kernel, grid=(STRIPS // PLACED,), out_shape=(jax.Sha...  4.06 us

profile of v9, /device:TPU:1, one launch (start us, length us, event | category | flops | bytes accessed | tf_op | source)
XLA Modules:
  0.0 98.5 jit_solution(277097586007440516)
XLA Ops:
  0.6 93.8 %windows.1 = (bf16[944,1024]{1,0:T(8,128)(2,1)}, bf16[128,1024]{1,0:T(8,128)(2,1)}, f32[4,2,16,256]{3,2,1,0:T(8,128)}) custom-call(bf16[864,1024]{1,0:T(8,128)(2,1)} %bitcast.3, bf16[864,1024]{1,0:T(8,128)(2,1)} %bitcast.4, bf16[1024,3072]{1,0:T(8,128)(2,1)} %w_qkv_hbm.1, bf16[1024,1024]{1,0:T(8,128)(2,1)} %w_out_hbm.1, s32[288]{0:T(512)} %row_valid.1), custom_call_target="tpu_custom_call" | custom-call | tf_op jit(solution)/shard_map/windows/pallas_call | solution.py:409
  94.5 4.1 %assembly.1 = (bf16[864,1024]{1,0:T(8,128)(2,1)}, f32[8,3072]{1,0:T(8,128)}, f32[8,1024]{1,0:T(8,128)}) custom-call(bf16[944,1024]{1,0:T(8,128)(2,1)} %get-tuple-element.9.d_ext.d_next, bf16[944,1024]{1,0:T(8,128)(2,1)} %get-tuple-element.9.d_ext.d_next, bf16[128,1024]{1,0:T(8,128)(2,1)} %get-tuple-element.10.d_edges, f32[4,2,16,256]{3,2,1,0:T(8,128)} %get-tuple-element.11.sum_3), custom_call_target="tpu_custom_call" | custom-call | tf_op jit(solution)/shard_map/assembly/pallas_call | solution.py:379
